TPU v7x, 128 devices: a whole 4x4x4 slice. The times are simulated.
128 devices in a mesh: group: 8 (over z_hi, x), domain: 16 (over y, z_lo, core).
Axes of the slice: x: 4, y: 4, z: 4 (z_hi: 2, z_lo: 2; z = z_hi * 2 + z_lo), core: 2. Of those that a mesh axis runs over, the one named last changes fastest.
Arguments:
- weight: float32 [8192, 7168], P(('group', 'domain')), may hold values from -6 to 6
- moment1: float32 [8192, 7168], P(('group', 'domain')), may hold values from -4 to 4
- moment2: float32 [8192, 7168], P(('group', 'domain')), may hold values from 0.01 to 1
- gradient: bfloat16 [8192, 7168], P(('group', 'domain')), may hold values from -6 to 6
- owner_table: int32 [16, 8], replicated, may hold values from 0 to 7, each once within a row
- exponents: int32 [8], replicated, may hold values from 0 to 7, each once
Outputs:
- weight_new: float32 [8192, 7168], P(('group', 'domain'))
- moment1_new: float32 [8192, 7168], P(('group', 'domain'))
- moment2_new: float32 [8192, 7168], P(('group', 'domain'))
- buddy_copy: float32 [8192, 3, 7168], P(('group', 'domain'))
- parity: float32 [1024, 3, 7168], P(('group', 'domain'))
Inputs may be any that keep to these rules, and one draw needn't show every extreme that they name: Each row of owner_table names every member once. `exponents`: every member has a different exponent.
All inputs are finite; a program needn't handle non-finite values.
Results may differ from a plain program's by a relative error of at most 0.0003.
Values sent between devices are 32-bit elements; how exact they have to be, the bound alone decides.
A program may use at most 128 MiB of HBM per device.

v0:
```python
import jax
import jax.numpy as jnp
from jax import lax
from jax.sharding import PartitionSpec as P

beta_one = 0.9
beta_two = 0.95
learning_rate = 0.02
weight_decay = 0.1
epsilon = 1e-08
step_count = 100.0


def from_behind(block, axis, distance):
    devices = range(lax.axis_size(axis))
    route = [((i - distance) % len(devices), i) for i in devices]
    return lax.ppermute(block, axis, route)


def adamw(weight, moment1, moment2, gradient):
    grad_float = gradient.astype(jnp.float32)
    first = beta_one * moment1 + (1.0 - beta_one) * grad_float
    second = beta_two * moment2 + (1.0 - beta_two) * grad_float * grad_float
    correct_one = 1.0 - beta_one**step_count
    correct_two = 1.0 - beta_two**step_count
    update = (
        first / correct_one / (jnp.sqrt(second / correct_two) + epsilon) + weight_decay * weight
    )
    return (weight - learning_rate * update, first, second)


def shards(weight, moment1, moment2, gradient, owner_table, exponents):
    members = lax.axis_size("group")
    member_index = lax.axis_index("group")
    domain_index = lax.axis_index("domain")
    buddy_stride = lax.axis_size("domain") // 4
    weight_new, moment1_new, moment2_new = adamw(weight, moment1, moment2, gradient)
    packed = jnp.stack([weight_new, moment1_new, moment2_new], axis=1)
    buddy_copy = from_behind(packed, "domain", buddy_stride)
    rows_local = weight.shape[0]
    stripe_rows = rows_local // members
    my_owners = lax.dynamic_index_in_dim(owner_table, domain_index, 0, keepdims=False)
    member_ids = jnp.arange(members)
    inverse = jnp.sum(
        jnp.where(my_owners[None, :] == member_ids[:, None], member_ids[None, :], 0), axis=1
    )
    points = 1.0 + (2.0 * jnp.arange(members).astype(jnp.float32) + 1.0 - members) / (4.0 * members)
    exponent_float = exponents.astype(jnp.float32)
    my_exponent = lax.dynamic_index_in_dim(exponent_float, member_index, 0, keepdims=False)
    scales = jnp.power(jnp.take(points, inverse), my_exponent)
    positions = jnp.arange(lax.axis_size("group") * stripe_rows)
    owners_of = positions // stripe_rows
    sources = jnp.take(inverse, owners_of) * stripe_rows + positions % stripe_rows
    selected = jnp.take(packed, sources, axis=0)
    parity = lax.psum_scatter(
        selected * jnp.take(scales, owners_of)[:, None, None],
        "group",
        scatter_dimension=0,
        tiled=True,
    )
    return (weight_new, moment1_new, moment2_new, buddy_copy, parity)


def solution(mesh):
    placed = (
        P(("group", "domain"), None),
        P(("group", "domain"), None),
        P(("group", "domain"), None),
        P(("group", "domain"), None),
        P(),
        P(),
    )
    return jax.shard_map(
        shards,
        mesh=mesh,
        in_specs=placed,
        out_specs=(
            P(("group", "domain"), None),
            P(("group", "domain"), None),
            P(("group", "domain"), None),
            P(("group", "domain"), None, None),
            P(("group", "domain"), None, None),
        ),
        check_vma=False,
    )
```

profile of v0, /device:TPU:0, one launch (start us, length us, event | category | flops | bytes accessed | tf_op | source)
XLA Modules:
  0.0 241.8 jit_solution(10050605228687610117)
XLA Ops:
  7.2 0.0 copy-start
  7.2 0.0 all-reduce.3.cloned.1.call-start
  7.2 0.6 copy-done
  7.9 0.2 dynamic-slice_reduce_fusion
  8.0 0.1 select_reduce_fusion
  8.2 0.7 fusion.13
  8.9 0.7 convert_element_type.11
  9.5 5.1 %compare_and_fusion = (pred[64]{0:T(512)(128)(4,1)S(1)}, s32[64]{0:T(128)S(1)}) fusion(s32[]{:T(128)} %bitcast.10, s32[]{:T(128)} %bitcast.9, s32[]{:T(128)} %bitcast.8, s32[]{:T(128)} %bitcast.7, s32[]{:T(128)} %bitcast.6, s32[]{:T(128)} %bitcast.5, s32[]{:T(128)} %bitcast.4, s32[]{:T(128)} %bitcast.3), kind=kLoop, calls=%fused_computation.25 | loop fusion | flops 3328 | bytes 352 | tf_op jit(solution)/shard_map/jit(_take)/and | solution.py:54
  14.7 0.6 dynamic_slice.9
  15.3 0.6 gather_fusion.1
  15.9 0.7 fusion.9
  16.6 0.7 fusion.12
  17.3 4.3 %multiply_subtract_fusion = (f32[64,7168]{1,0:T(8,128)S(1)}, f32[64,7168]{1,0:T(8,128)S(1)}, f32[64,7168]{1,0:T(8,128)S(1)}) fusion(f32[64,7168]{1,0:T(8,128)} %param.6, bf16[64,7168]{1,0:T(8,128)(2,1)} %param.9, f32[64,7168]{1,0:T(8,128)} %param.7, f32[64,7168]{1,0:T(8,128)} %param.8), kind=kLoop, calls=%fused_computation.8 | loop fusion | flops 7340032 | bytes 11927552 | tf_op jit(solution)/shard_map/sub | solution.py:29
  21.6 0.0 copy-start.2
  21.6 0.0 copy-start.1
  21.6 0.0 copy-start.3
  21.6 1.9 copy.20
  23.5 0.0 copy-done.2
  23.6 0.0 copy-done.1
  23.6 1.9 copy.19
  25.5 0.0 copy-done.3
  25.5 1.3 stack.14
  26.7 6.4 %pad_maximum_fusion = f32[64,3,7168]{2,1,0:T(4,128)} fusion(f32[64,1,7168]{2,1,0:T(1,128)S(1)} %stack.14, f32[64,1,7168]{2,1,0:T(1,128)S(1)} %copy.20, f32[64,1,7168]{2,1,0:T(1,128)S(1)} %copy.19), kind=kLoop, calls=%fused_computation.2 | loop fusion | flops 2752512 | bytes 11010048 | tf_op jit(solution)/shard_map/stack | solution.py:38
  33.1 10.6 %gather_fusion = f32[64,3,7168]{2,1,0:T(4,128)} fusion(f32[64,3,7168]{2,1,0:T(4,128)} %pad_maximum_fusion, s32[1024]{0:T(1024)S(1)} %pad_clamp_fusion.1), kind=kCustom, calls=%fused_computation | custom fusion | bytes 11010304 | tf_op jit(solution)/shard_map/jit(_take)/gather | solution.py:54
  43.7 5.2 %fusion.5 = f32[64]{0:T(128)S(1)} fusion(f32[]{:T(128)} %bitcast.18, f32[]{:T(128)} %bitcast.19, f32[]{:T(128)} %bitcast.20, f32[]{:T(128)} %bitcast.21, f32[]{:T(128)} %bitcast.22, f32[]{:T(128)} %bitcast.24, f32[]{:T(128)} %bitcast.23, f32[]{:T(128)} %bitcast.17), kind=kLoop, calls=%fused_computation.51 | loop fusion | flops 2560 | bytes 288 | tf_op jit(solution)/shard_map/jit(_take)/select_n | solution.py:56
  48.9 9.1 %select_multiply_fusion = f32[64,3,7168]{2,1,0:T(4,128)} fusion(f32[64,3,7168]{2,1,0:T(4,128)} %gather_fusion, f32[64]{0:T(128)S(1)} %fusion.5, pred[64]{0:T(512)(128)(4,1)S(1)} %get-tuple-element.20), kind=kLoop, calls=%fused_computation.3 | loop fusion | flops 2752512 | bytes 11010368 | tf_op jit(solution)/shard_map/mul | solution.py:56
  58.0 0.0 all-reduce.3.cloned.1.call-update
  58.0 0.0 copy-start.4
  58.0 8.7 %copy.21 = f32[64,3,7168]{2,0,1:T(8,128)} copy(f32[64,3,7168]{2,1,0:T(4,128)} %pad_maximum_fusion) | data formatting | bytes 11010048 | tf_op jit(solution)/shard_map/stack | solution.py:38
  66.8 1.7 collective-permute-start
  68.4 0.0 copy-done.4
  68.4 0.6 dynamic-slice
  69.7 157.1 %all-reduce.3.cloned.1.call-done = f32[64,3,7168]{2,1,0:T(4,128)} async-done(((f32[64,3,7168]{2,1,0:T(4,128)}), f32[64,3,7168]{2,1,0:T(4,128)}) %all-reduce.3.cloned.1.call-update) | async-done | bytes 5505040
  226.8 1.3 constant_dynamic-slice_fusion
  228.2 1.2 copy.22
  229.4 0.0 collective-permute-done
  229.4 5.5 %copy.25 = f32[64,3,7168]{2,0,1:T(8,128)} copy(f32[64,3,7168]{2,0,1:T(8,128)} %collective-permute-done) | data formatting | bytes 11010048
  (5 shorter events, 0.0 us)
Async XLA Ops:
  7.2 0.7 copy-start
  7.2 219.6 %all-reduce.3.cloned.1.call-start = ((), (), s32[]{:S(2)}) async-start(), calls=%async_computation | async-start | bytes 14680064
  21.6 1.9 copy-start.2
  21.6 1.9 copy-start.1
  21.6 3.8 %copy-start.3 = (f32[64,7168]{1,0:T(8,128)}, f32[64,7168]{1,0:T(8,128)S(1)}, u32[]{:S(2)}) copy-start(f32[64,7168]{1,0:T(8,128)S(1)} %get-tuple-element.48) | copy-start | bytes 5505028
  58.0 10.4 %copy-start.4 = (u32[128]{0:T(128)S(1)}, u32[128]{0:T(128)}, u32[]{:S(2)}) copy-start(u32[128]{0:T(128)} %constant.163) | copy-start | bytes 1540
  66.8 162.7 %collective-permute-start = (f32[64,3,7168]{2,0,1:T(8,128)}, f32[64,3,7168]{2,0,1:T(8,128)}, u32[]{:S(2)}, u32[]{:S(2)}) collective-permute-start(f32[64,3,7168]{2,0,1:T(8,128)} %copy.21), channel_id=1, source_target_pairs={{12,0},{13,1},{14,2},{15,3},{0,4},{1,5},{2,6},{3,7},{4,8},{5,9},{6... | collective-permute-start | bytes 16515080 | tf_op jit(solution)/shard_map/ppermute | solution.py:17
Sparse Core Ops, SparseCore 0:
  58.1 168.6 all-reduce.2
where the time goes:
time: 243 us; the launch traced here: 242 us
  waiting for transfers between devices  157 us (65%)
  local copies, waits for them, and re-layouts  36.5 us (15%)
  other arithmetic  31.6 us (13%)
  between operations  14.8 us (6%)
    unnamed x2, waiting for transfers between devices  157 us
    another operation x4, local copies, waits for them, and re-layouts, shards(): packed = jnp.stack([weight_new, moment1_new, moment2_new], axis=1)  13.8 us
    gather x1, local copies, waits for them, and re-layouts, shards(): selected = jnp.take(packed, sources, axis=0)  10.6 us
    unnamed x14, local copies, waits for them, and re-layouts  9.35 us
    mul x1, other arithmetic, shards(): selected * jnp.take(scales, owners_of)[:, None, None]  9.06 us
    another operation x1, other arithmetic, shards(): packed = jnp.stack([weight_new, moment1_new, moment2_new], axis=1)  6.41 us
    select_n x1, other arithmetic, shards(): jnp.take(scales, owners_of)[:, None, None]  5.21 us
    and x1, other arithmetic, shards(): selected = jnp.take(packed, sources, axis=0)  5.12 us
  transfers between devices with their start and end apart: 2, of which 1 were waited for; matrix products, arithmetic and copies ran while one was open for 5% of the time, Pallas kernels for 0%

commit v1 on v0

v1 whole, which is shorter than its diff:
```python
import functools

import jax
import jax.numpy as jnp
from jax import lax
from jax.experimental import pallas as pl
from jax.experimental.pallas import tpu as pltpu
from jax.sharding import PartitionSpec as P

beta_one = 0.9
beta_two = 0.95
learning_rate = 0.02
weight_decay = 0.1
epsilon = 1e-08
step_count = 100.0

MESH = pl.DeviceIdType.MESH
XS, ZHS, YS, ZLS, CORES = 4, 2, 4, 2, 2
STRIPE = 8
LONG_STRIPES = 2


def adamw(weight, moment1, moment2, gradient):
    grad_float = gradient.astype(jnp.float32)
    first = beta_one * moment1 + (1.0 - beta_one) * grad_float
    second = beta_two * moment2 + (1.0 - beta_two) * grad_float * grad_float
    correct_one = 1.0 - beta_one**step_count
    correct_two = 1.0 - beta_two**step_count
    update = (
        first / correct_one / (jnp.sqrt(second / correct_two) + epsilon) + weight_decay * weight
    )
    return (weight - learning_rate * update, first, second)


def coefficient(stripe, exponent):
    bits = [(jnp.right_shift(exponent, i) & 1).astype(jnp.float32) for i in range(3)]
    point = 1.0 + (2.0 * stripe.astype(jnp.float32) - 7.0) / 32.0
    square = point * point
    fourth = square * square
    power = 1.0
    for bit, factor in zip(bits, (point, square, fourth)):
        power = power * (1.0 + bit * (factor - 1.0))
    return power


def same(a, b):
    gap = a - b
    return 1 - jnp.minimum(jnp.maximum(gap, -gap), 1)


def exchange_kernel(
    owner_ref, exponent_ref, w_ref, m_ref, v_ref, buddy_ref, parity_ref,
    held, scaled, arrived, total, hop1, hop2,
    load_sem, plus_send, plus_recv, hop_send, hop_recv, piece_send, piece_recv, out_sem,
):
    group = lax.axis_index("group")
    domain = lax.axis_index("domain")
    x = group % XS
    zh = group // XS
    per_y = ZLS * CORES
    y_plus = (domain + per_y) % (YS * per_y)
    y_minus = (domain + (YS - 1) * per_y) % (YS * per_y)
    arrays = (w_ref, m_ref, v_ref)
    stripes = w_ref.shape[0]
    short = stripes - LONG_STRIPES

    offsets = [(dx, dz) for dz in range(ZHS) for dx in range(XS)]
    partners = [((zh + dz) % ZHS) * XS + (x + dx) % XS for dx, dz in offsets]

    loads = []
    for a in range(3):
        load = pltpu.make_async_copy(arrays[a], held.at[a], load_sem.at[a])
        load.start()
        loads.append(load)

    barrier = pltpu.get_barrier_semaphore()
    for other in (y_plus, y_minus):
        pl.semaphore_signal(barrier, inc=1, device_id=(group, other), device_id_type=MESH)
    for partner in partners[1:]:
        pl.semaphore_signal(barrier, inc=1, device_id=(partner, domain), device_id_type=MESH)
    pl.semaphore_wait(barrier, 2 + len(partners) - 1)

    plus = []
    for a in range(3):
        copy = pltpu.make_async_remote_copy(
            src_ref=arrays[a].at[pl.ds(0, short)],
            dst_ref=buddy_ref.at[a, pl.ds(0, short)],
            send_sem=plus_send.at[a],
            recv_sem=plus_recv.at[a],
            device_id=(group, y_plus),
            device_id_type=MESH,
        )
        copy.start()
        plus.append(copy)

    chunks = [(a, r) for r in range(LONG_STRIPES) for a in range(3)]

    def hop(step, i):
        a, r = chunks[i]
        source = (arrays[a].at[short + r], hop1.at[i], hop2.at[i])[step]
        target = (hop1.at[i], hop2.at[i], buddy_ref.at[a, short + r])[step]
        return pltpu.make_async_remote_copy(
            src_ref=source,
            dst_ref=target,
            send_sem=hop_send.at[step, i],
            recv_sem=hop_recv.at[step, i],
            device_id=(group, y_minus),
            device_id_type=MESH,
        )

    for i in range(len(chunks)):
        hop(0, i).start()

    exponent = exponent_ref[group]
    for load in loads:
        load.wait()

    def stripe_of(owner):
        stripe = jnp.int32(0)
        for s in range(stripes):
            stripe = stripe + s * same(owner_ref[domain, s], owner)
        return jnp.minimum(stripe, stripes - 1)

    pieces = []
    for slot in [1, 3, 4, 2, 5, 7, 6, 0]:
        stripe = stripe_of(partners[slot])
        scale = coefficient(stripe, exponent)
        for a in range(3):
            scaled[slot, a] = held[a, stripe] * scale
        if slot:
            piece = pltpu.make_async_remote_copy(
                src_ref=scaled.at[slot],
                dst_ref=arrived.at[slot - 1],
                send_sem=piece_send.at[slot - 1],
                recv_sem=piece_recv.at[slot - 1],
                device_id=(partners[slot], domain),
                device_id_type=MESH,
            )
            piece.start()
            pieces.append(piece)

    for step in range(2):
        for i in range(len(chunks)):
            hop(step, i).wait_recv()
            hop(step + 1, i).start()

    total[...] = scaled[0]
    for slot, piece in zip([1, 3, 4, 2, 5, 7, 6], pieces):
        piece.wait_recv()
        total[...] += arrived[slot - 1]
    out = pltpu.make_async_copy(total, parity_ref, out_sem)
    out.start()

    for i in range(len(chunks)):
        hop(2, i).wait_recv()
    for copy in plus:
        copy.wait()
    for step in range(3):
        for i in range(len(chunks)):
            hop(step, i).wait_send()
    for piece in pieces:
        piece.wait_send()
    out.wait()


def exchange(owner_table, exponents, w, m, v):
    members = XS * ZHS
    stripes, width = w.shape[0] // STRIPE, w.shape[1]
    chunks = 3 * LONG_STRIPES
    w, m, v = (a.reshape(stripes, STRIPE, width) for a in (w, m, v))
    smem = pl.BlockSpec(memory_space=pltpu.SMEM)
    anywhere = pl.BlockSpec(memory_space=pl.ANY)
    f32 = jnp.float32
    dma = pltpu.SemaphoreType.DMA
    return pl.pallas_call(
        exchange_kernel,
        out_shape=(
            jax.ShapeDtypeStruct((3, stripes, STRIPE, width), f32),
            jax.ShapeDtypeStruct((3, STRIPE, width), f32),
        ),
        in_specs=[smem, smem, anywhere, anywhere, anywhere],
        out_specs=(anywhere, anywhere),
        scratch_shapes=[
            pltpu.VMEM((3, stripes, STRIPE, width), f32),
            pltpu.VMEM((members, 3, STRIPE, width), f32),
            pltpu.VMEM((members - 1, 3, STRIPE, width), f32),
            pltpu.VMEM((3, STRIPE, width), f32),
            pltpu.VMEM((chunks, STRIPE, width), f32),
            pltpu.VMEM((chunks, STRIPE, width), f32),
            dma((3,)),
            dma((3,)),
            dma((3,)),
            dma((3, chunks)),
            dma((3, chunks)),
            dma((members - 1,)),
            dma((members - 1,)),
            dma,
        ],
        compiler_params=pltpu.CompilerParams(
            collective_id=0, has_side_effects=True, vmem_limit_bytes=40 << 20
        ),
        name="exchange",
    )(owner_table, exponents, w, m, v)


def shards(weight, moment1, moment2, gradient, owner_table, exponents):
    w, m, v = adamw(weight, moment1, moment2, gradient)
    buddy, parity = exchange(owner_table, exponents, w, m, v)
    buddy = buddy.reshape(3, -1, buddy.shape[-1])
    return (w, m, v, jnp.transpose(buddy, (1, 0, 2)), jnp.transpose(parity, (1, 0, 2)))


def solution(mesh):
    rows = P(("group", "domain"), None)
    blocks = P(("group", "domain"), None, None)
    return jax.shard_map(
        shards,
        mesh=mesh,
        in_specs=(rows, rows, rows, rows, P(), P()),
        out_specs=(rows, rows, rows, blocks, blocks),
        check_vma=False,
    )
```

time: 243 us -> 109 us (0.45)
  waiting for transfers between devices: 157 us -> 0 us
  Pallas kernels: 0 us -> 100 us
  local copies, waits for them, and re-layouts: 36.5 us -> 4.07 us
  other arithmetic: 31.6 us -> 4.34 us
  between operations: 14.8 us -> 0.7 us
    unnamed x2 -> x0, waiting for transfers between devices: 157 us -> none
    pallas_call x0 -> x1, Pallas kernels: none -> 100 us  [exchange(): pl.pallas_call(exchange_kernel, out_shape=(jax.ShapeDtypeStruct((3, strip...]
    another operation x4 -> x0, local copies, waits for them, and re-layouts: 13.8 us -> none  [shards(): packed = jnp.stack([weight_new, moment1_new, moment2_new], axis=1)]
    gather x4 -> x0, local copies, waits for them, and re-layouts: 12.6 us -> none  [the longest x1 10.6 us: shards(): selected = jnp.take(packed, sources, axis=0)]
    mul x1 -> x0, other arithmetic: 9.06 us -> none  [shards(): selected * jnp.take(scales, owners_of)[:, None, None]]
    another operation x1 -> x0, other arithmetic: 6.41 us -> none  [shards(): packed = jnp.stack([weight_new, moment1_new, moment2_new], axis=1)]
    unnamed x14 -> x11, local copies, waits for them, and re-layouts: 9.35 us -> 4.07 us
    select_n x3 -> x0, other arithmetic: 5.23 us -> none  [the longest x1 5.21 us: shards(): jnp.take(scales, owners_of)[:, None, None]]
  transfers between devices with their start and end apart: 2 -> 0, of which waited for: 1 -> 0; matrix products, arithmetic and copies ran while one was open for 5% -> 0% of each run, Pallas kernels for 0% -> 0%
where the time goes in v1:
time: 109 us
  Pallas kernels  100 us (92%)
  other arithmetic  4.34 us (4%)
  local copies, waits for them, and re-layouts  4.07 us (4%)
    pallas_call x1, Pallas kernels, exchange(): pl.pallas_call(exchange_kernel, out_shape=(jax.ShapeDtypeStruct((3, strip...  100 us
    sub x1, other arithmetic, adamw(): return (weight - learning_rate * update, first, second)  4.34 us
    unnamed x11, local copies, waits for them, and re-layouts  4.07 us

profile of v1, /device:TPU:0, one launch (start us, length us, event | category | flops | bytes accessed | tf_op | source)
XLA Modules:
  0.0 109.2 jit_solution(13563396333266441407)
XLA Ops:
  0.6 0.8 copy.11.owner_ref
  1.4 0.0 copy-start.3
  1.4 4.3 %multiply_subtract_fusion = (f32[64,7168]{1,0:T(8,128)S(1)}, f32[64,7168]{1,0:T(8,128)S(1)}, f32[64,7168]{1,0:T(8,128)S(1)}) fusion(f32[64,7168]{1,0:T(8,128)} %param.6, bf16[64,7168]{1,0:T(8,128)(2,1)} %param.9, f32[64,7168]{1,0:T(8,128)} %param.7, f32[64,7168]{1,0:T(8,128)} %param.8), kind=kLoop, calls=%fused_computation.4 | loop fusion | flops 7340032 | bytes 11927552 | tf_op jit(solution)/shard_map/sub | solution.py:32
  5.7 0.0 copy-start
  5.7 0.0 copy-start.1
  5.8 0.0 copy-start.2
  5.8 0.0 copy-done.3
  5.8 100.1 %exchange.1 = (f32[3,8,8,7168]{3,2,1,0:T(8,128)S(1)}, f32[3,8,7168]{2,1,0:T(8,128)S(1)}) custom-call(s32[16,8]{1,0:T(8,128)S(1)} %copy.11.owner_ref, s32[8]{0:T(128)S(1)} %copy-done.3, f32[8,8,7168]{2,1,0:T(8,128)S(1)} %bitcast.7, f32[8,8,7168]{2,1,0:T(8,128)S(1)} %bitcast.8, f32[8,8,7168]{2,1,0:T(8,128)S(1)} %bitcast.9), custom_call_target="tpu_custom_call" | custom-call | tf_op jit(solution)/shard_map/exchange/pallas_call | solution.py:175
  105.9 0.0 copy-done
  105.9 0.0 copy-done.1
  105.9 0.0 copy-done.2
  105.9 2.4 %copy.14 = f32[64,3,7168]{2,0,1:T(8,128)} copy(f32[64,3,7168]{2,0,1:T(8,128)S(1)} %bitcast.10) | data formatting | bytes 11010048
  108.4 0.8 copy.15
Async XLA Ops:
  1.4 4.4 %copy-start.3 = (s32[8]{0:T(128)S(1)}, s32[8]{0:T(128)}, u32[]{:S(2)}) copy-start(s32[8]{0:T(128)} %exponent_ref.1) | copy-start | bytes 100
  5.7 100.2 %copy-start = (f32[64,7168]{1,0:T(8,128)}, f32[64,7168]{1,0:T(8,128)S(1)}, u32[]{:S(2)}) copy-start(f32[64,7168]{1,0:T(8,128)S(1)} %get-tuple-element.17) | copy-start | bytes 5505028
  5.7 100.2 %copy-start.1 = (f32[64,7168]{1,0:T(8,128)}, f32[64,7168]{1,0:T(8,128)S(1)}, u32[]{:S(2)}) copy-start(f32[64,7168]{1,0:T(8,128)S(1)} %get-tuple-element.18) | copy-start | bytes 5505028
  5.8 100.2 %copy-start.2 = (f32[64,7168]{1,0:T(8,128)}, f32[64,7168]{1,0:T(8,128)S(1)}, u32[]{:S(2)}) copy-start(f32[64,7168]{1,0:T(8,128)S(1)} %get-tuple-element.19) | copy-start | bytes 5505028

commit v2 on v0

v2 whole, which is shorter than its diff:
```python
import jax
import jax.numpy as jnp
from jax import lax
from jax.experimental import pallas as pl
from jax.experimental.pallas import tpu as pltpu
from jax.sharding import PartitionSpec as P

beta_one = 0.9
beta_two = 0.95
learning_rate = 0.02
weight_decay = 0.1
epsilon = 1e-08
step_count = 100.0

MESH = pl.DeviceIdType.MESH
XS, ZS, YS, ZLS, CORES = 4, 4, 4, 2, 2
ZHS = ZS // ZLS
STRIPE = 8
LONG_STRIPES = 2
F32 = jnp.float32
DMA = pltpu.SemaphoreType.DMA
IN_HBM = pl.BlockSpec(memory_space=pltpu.HBM)
IN_VMEM = pl.BlockSpec(memory_space=pltpu.VMEM)


def adamw(weight, moment1, moment2, gradient):
    grad_float = gradient.astype(F32)
    first = beta_one * moment1 + (1.0 - beta_one) * grad_float
    second = beta_two * moment2 + (1.0 - beta_two) * grad_float * grad_float
    correct_one = 1.0 - beta_one**step_count
    correct_two = 1.0 - beta_two**step_count
    update = (
        first / correct_one / (jnp.sqrt(second / correct_two) + epsilon) + weight_decay * weight
    )
    return (weight - learning_rate * update, first, second)


def coefficient(stripe, exponent):
    bits = [(jnp.right_shift(exponent, i) & 1).astype(F32) for i in range(3)]
    point = 1.0 + (2.0 * stripe.astype(F32) - 7.0) / 32.0
    square = point * point
    fourth = square * square
    power = 1.0
    for bit, factor in zip(bits, (point, square, fourth)):
        power = power * (1.0 + bit * (factor - 1.0))
    return power


def same(a, b):
    gap = a - b
    return 1 - jnp.minimum(jnp.maximum(gap, -gap), 1)


def exchange_kernel(
    owners_in, exponents_in, w_in, m_in, v_in, g_in, fresh, buddy_ref, parity_ref,
    w, m, v, g, owner_ref, exponent_ref, scaled, first_in, second_in, relay, across, hop1, hop2,
    load_sem, table_sem, plus_send, plus_recv, hop_send, hop_recv, x_send, x_recv, z_send, z_recv,
):
    group = lax.axis_index("group")
    domain = lax.axis_index("domain")
    x, zh = group % XS, group // XS
    core, zl, y = domain % CORES, (domain // CORES) % ZLS, domain // (CORES * ZLS)
    z = zh * ZLS + zl

    def device(x, y, z):
        return ((z // ZLS) * XS + x, (y * ZLS + z % ZLS) * CORES + core)

    y_plus, y_minus = device(x, (y + 1) % YS, z), device(x, (y + YS - 1) % YS, z)
    x_plus, x_minus = device((x + 1) % XS, y, z), device((x + XS - 1) % XS, y, z)
    z_plus, z_minus = device(x, y, (z + 1) % ZS), device(x, y, (z + ZS - 1) % ZS)
    stripes = w.shape[0]
    short = stripes - LONG_STRIPES
    half = w.shape[2] // 2

    tables = [
        pltpu.make_async_copy(owners_in, owner_ref, table_sem.at[0]),
        pltpu.make_async_copy(exponents_in, exponent_ref, table_sem.at[1]),
    ]

    def loads(pair):
        two, rows = pl.ds(2 * pair, 2), pl.ds(2 * STRIPE * pair, 2 * STRIPE)
        ends = [(w_in.at[two], w.at[two]), (m_in.at[two], m.at[two]), (v_in.at[two], v.at[two])]
        ends.append((g_in.at[rows], g.at[rows]))
        return [pltpu.make_async_copy(*e, load_sem.at[pair, i]) for i, e in enumerate(ends)]

    pairs = [stripes // 2 - 1, *range(stripes // 2 - 1)]
    for pair in pairs:
        for load in loads(pair):
            load.start()

    def send(source, target, send_sem, recv_sem, to):
        return pltpu.make_async_remote_copy(
            src_ref=source,
            dst_ref=target,
            send_sem=send_sem,
            recv_sem=recv_sem,
            device_id=to,
            device_id_type=MESH,
        )

    barrier = pltpu.get_barrier_semaphore()
    neighbours = (y_plus, y_minus, x_plus, x_minus, z_plus, z_minus)
    for other in neighbours:
        pl.semaphore_signal(barrier, inc=1, device_id=other, device_id_type=MESH)
    for table in tables:
        table.start()

    def update(pair):
        for load in loads(pair):
            load.wait()
        gradient = g[pl.ds(2 * STRIPE * pair, 2 * STRIPE), :].astype(F32)
        for h in range(2):
            s = 2 * pair + h
            fresh[0, s], fresh[1, s], fresh[2, s] = adamw(
                w[s], m[s], v[s], gradient[h * STRIPE : (h + 1) * STRIPE]
            )

    def plus(s):
        return send(fresh.at[:, s], buddy_ref.at[:, s], plus_send.at[s], plus_recv.at[s], y_plus)

    chunks = [(a, short + r) for r in range(LONG_STRIPES) for a in range(3)]

    def hop(step, i):
        a, s = chunks[i]
        source = (fresh.at[a, s], hop1.at[i], hop2.at[i])[step]
        target = (hop1.at[i], hop2.at[i], buddy_ref.at[a, s])[step]
        return send(source, target, hop_send.at[step, i], hop_recv.at[step, i], y_minus)

    update(pairs[0])
    update(pairs[1])
    pl.semaphore_wait(barrier, len(neighbours))
    for i in range(len(chunks)):
        hop(0, i).start()
        if i < 2:
            plus(2 * pairs[1] + i).start()
    for pair in pairs[2:]:
        update(pair)
        plus(2 * pair).start()
        plus(2 * pair + 1).start()

    for table in tables:
        table.wait()
    exponent = exponent_ref[group]

    def scale(dx, dz):
        owner = ((zh + dz) % ZHS) * XS + (x + dx) % XS
        stripe = jnp.int32(0)
        for s in range(stripes):
            stripe = stripe + s * same(owner_ref[s, domain], owner)
        stripe = jnp.minimum(stripe, stripes - 1)
        factor = coefficient(stripe, exponent)
        for a in range(3):
            scaled[dz * XS + dx, a] = fresh[a, stripe] * factor

    def along_x(i, slot, target, to):
        return send(scaled.at[slot], target, x_send.at[i], x_recv.at[i], to)

    far_plus = along_x(0, 2, first_in.at[0], x_plus)
    far_minus = along_x(1, XS + 2, first_in.at[1], x_minus)
    near_plus = along_x(2, XS + 1, second_in.at[0], x_plus)
    near_minus = along_x(3, XS - 1, second_in.at[1], x_minus)
    sum_plus = along_x(4, 1, second_in.at[2], x_plus)
    sum_minus = along_x(5, XS + XS - 1, second_in.at[3], x_minus)
    scale(2, 0)
    far_plus.start()
    scale(2, 1)
    far_minus.start()
    scale(1, 1)
    near_plus.start()
    scale(3, 0)
    near_minus.start()
    scale(1, 0)
    scale(3, 1)
    scale(0, 0)
    scale(0, 1)

    far_plus.wait_recv()
    scaled[1] += first_in[0]
    sum_plus.start()
    far_minus.wait_recv()
    scaled[XS + XS - 1] += first_in[1]
    sum_minus.start()

    for i in range(len(chunks)):
        hop(0, i).wait_recv()
        hop(1, i).start()

    for copy in (near_plus, near_minus, sum_plus, sum_minus):
        copy.wait_recv()
    scaled[XS] += second_in[0] + second_in[3]
    left, right = pl.ds(0, half), pl.ds(half, half)
    out_plus = send(scaled.at[XS, :, :, left], relay.at[0], z_send.at[0], z_recv.at[0], z_plus)
    out_minus = send(scaled.at[XS, :, :, right], relay.at[1], z_send.at[1], z_recv.at[1], z_minus)
    on_plus = send(relay.at[0], across.at[0], z_send.at[2], z_recv.at[2], z_plus)
    on_minus = send(relay.at[1], across.at[1], z_send.at[3], z_recv.at[3], z_minus)
    out_plus.start()
    out_minus.start()
    parity_ref[...] = scaled[0] + second_in[1] + second_in[2]
    out_plus.wait_recv()
    on_plus.start()
    out_minus.wait_recv()
    on_minus.start()

    for i in range(len(chunks)):
        hop(1, i).wait_recv()
        hop(2, i).start()

    on_plus.wait_recv()
    parity_ref[:, :, left] += across[0]
    on_minus.wait_recv()
    parity_ref[:, :, right] += across[1]

    for copy in (far_plus, far_minus, near_plus, near_minus, sum_plus, sum_minus):
        copy.wait_send()
    for copy in (out_plus, out_minus, on_plus, on_minus):
        copy.wait_send()
    for step in range(3):
        for i in range(len(chunks)):
            hop(step, i).wait_send()
    for s in range(short):
        plus(s).wait_send()
    for s in range(short):
        plus(s).wait_recv()
    for i in range(len(chunks)):
        hop(2, i).wait_recv()


def exchange(owners, exponents, w, m, v, g):
    shape = w.shape
    stripes, _, width = shape
    chunks = 3 * LONG_STRIPES
    block = (3, STRIPE, width)
    halves = (2, 3, STRIPE, width // 2)
    return pl.pallas_call(
        exchange_kernel,
        out_shape=(
            pltpu.VMEM((3, *shape), F32),
            pltpu.VMEM((3, *shape), F32),
            pltpu.VMEM(block, F32),
        ),
        in_specs=[IN_HBM] * 6,
        out_specs=(IN_VMEM,) * 3,
        scratch_shapes=[
            pltpu.VMEM(shape, F32),
            pltpu.VMEM(shape, F32),
            pltpu.VMEM(shape, F32),
            pltpu.VMEM(g.shape, g.dtype),
            pltpu.SMEM(owners.shape, jnp.int32),
            pltpu.SMEM(exponents.shape, jnp.int32),
            pltpu.VMEM((XS * ZHS, *block), F32),
            pltpu.VMEM((2, *block), F32),
            pltpu.VMEM((4, *block), F32),
            pltpu.VMEM(halves, F32),
            pltpu.VMEM(halves, F32),
            pltpu.VMEM((chunks, STRIPE, width), F32),
            pltpu.VMEM((chunks, STRIPE, width), F32),
            DMA((stripes // 2, 4)),
            DMA((2,)),
            DMA((stripes,)),
            DMA((stripes,)),
            DMA((3, chunks)),
            DMA((3, chunks)),
            DMA((6,)),
            DMA((6,)),
            DMA((4,)),
            DMA((4,)),
        ],
        compiler_params=pltpu.CompilerParams(
            collective_id=0, has_side_effects=True, vmem_limit_bytes=40 << 20
        ),
        name="exchange",
    )(owners, exponents, w, m, v, g)


def finish_kernel(fresh, buddy, parity, w_out, m_out, v_out, buddy_out, parity_out, sem):
    copies = [pltpu.make_async_copy(parity, parity_out, sem.at[0])]
    for a, out in enumerate((w_out, m_out, v_out)):
        copies.append(pltpu.make_async_copy(fresh.at[a], out, sem.at[1 + a]))
        copies.append(pltpu.make_async_copy(buddy.at[a], buddy_out.at[a], sem.at[4 + a]))
    for copy in copies:
        copy.start()
    for copy in copies:
        copy.wait()


def finish(fresh, buddy, parity):
    one = jax.ShapeDtypeStruct(fresh.shape[1:], F32)
    return pl.pallas_call(
        finish_kernel,
        out_shape=(
            one,
            one,
            one,
            jax.ShapeDtypeStruct(buddy.shape, F32),
            jax.ShapeDtypeStruct(parity.shape, F32),
        ),
        in_specs=[IN_VMEM] * 3,
        out_specs=(IN_HBM,) * 5,
        scratch_shapes=[DMA((7,))],
        compiler_params=pltpu.CompilerParams(vmem_limit_bytes=1 << 20),
        name="finish",
    )(fresh, buddy, parity)


def shards(weight, moment1, moment2, gradient, owner_table, exponents):
    rows, width = weight.shape
    w, m, v = (a.reshape(rows // STRIPE, STRIPE, width) for a in (weight, moment1, moment2))
    held = (owner_table.T, exponents, w, m, v, gradient)
    held = (pltpu.with_memory_space_constraint(a, pltpu.HBM) for a in held)
    fresh, buddy, parity = exchange(*held)
    w, m, v, buddy, parity = finish(fresh, buddy, parity)
    buddy = jnp.transpose(buddy.reshape(3, rows, width), (1, 0, 2))
    parity = jnp.transpose(parity, (1, 0, 2))
    return (*(a.reshape(rows, width) for a in (w, m, v)), buddy, parity)


def solution(mesh):
    rows = P(("group", "domain"), None)
    blocks = P(("group", "domain"), None, None)
    return jax.shard_map(
        shards,
        mesh=mesh,
        in_specs=(rows, rows, rows, rows, P(), P()),
        out_specs=(rows, rows, rows, blocks, blocks),
        check_vma=False,
    )
```

time: 243 us -> 102 us (0.42)
  waiting for transfers between devices: 157 us -> 0 us
  Pallas kernels: 0 us -> 101 us
  local copies, waits for them, and re-layouts: 36.5 us -> 0 us
  other arithmetic: 31.6 us -> 0 us
  between operations: 14.8 us -> 0.64 us
    unnamed x2 -> x0, waiting for transfers between devices: 157 us -> none
    pallas_call x0 -> x2, Pallas kernels: none -> 101 us  [the longest x1 97 us: exchange(): pl.pallas_call(exchange_kernel, out_shape=(pltpu.VMEM((3, *shape), F32),...]
    another operation x4 -> x0, local copies, waits for them, and re-layouts: 13.8 us -> none  [shards(): packed = jnp.stack([weight_new, moment1_new, moment2_new], axis=1)]
    gather x4 -> x0, local copies, waits for them, and re-layouts: 12.6 us -> none  [the longest x1 10.6 us: shards(): selected = jnp.take(packed, sources, axis=0)]
    unnamed x14 -> x0, local copies, waits for them, and re-layouts: 9.35 us -> none
    mul x1 -> x0, other arithmetic: 9.06 us -> none  [shards(): selected * jnp.take(scales, owners_of)[:, None, None]]
    another operation x1 -> x0, other arithmetic: 6.41 us -> none  [shards(): packed = jnp.stack([weight_new, moment1_new, moment2_new], axis=1)]
    select_n x3 -> x0, other arithmetic: 5.23 us -> none  [the longest x1 5.21 us: shards(): jnp.take(scales, owners_of)[:, None, None]]
  transfers between devices with their start and end apart: 2 -> 0, of which waited for: 1 -> 0; matrix products, arithmetic and copies ran while one was open for 5% -> 0% of each run, Pallas kernels for 0% -> 0%
where the time goes in v2:
time: 102 us
  Pallas kernels  101 us (99%)
    pallas_call x1, Pallas kernels, exchange(): pl.pallas_call(exchange_kernel, out_shape=(pltpu.VMEM((3, *shape), F32),...  97 us
    pallas_call x1, Pallas kernels, finish(): pl.pallas_call(finish_kernel, out_shape=(one, one, one, jax.ShapeDtypeStr...  4.38 us

profile of v2, /device:TPU:0, one launch (start us, length us, event | category | flops | bytes accessed | tf_op | source)
XLA Modules:
  0.0 102.0 jit_solution(15858323095384335851)
XLA Ops:
  0.6 97.0 %exchange.1 = (f32[3,8,8,7168]{3,2,1,0:T(8,128)S(1)}, f32[3,8,8,7168]{3,2,1,0:T(8,128)S(1)}, f32[3,8,7168]{2,1,0:T(8,128)S(1)}) custom-call(s32[8,16]{1,0:T(8,128)} %bitcast.14, s32[8]{0:T(128)} %exponents_in.1, f32[8,8,7168]{2,1,0:T(8,128)} %bitcast.11, f32[8,8,7168]{2,1,0:T(8,128)} %bitcast.12, f32[8,8,7168]{2,1,0:T(8,128)} %bitcast.13, bf16[64,7168]{1,0:T(8,128)(2,1)} %g_in.1), custom_call_target="tpu_custom_call" | custom-call | tf_op jit(solution)/shard_map/exchange/pallas_call | solution.py:234
  97.7 4.4 %finish.1 = (f32[8,8,7168]{2,1,0:T(8,128)}, f32[8,8,7168]{2,1,0:T(8,128)}, f32[8,8,7168]{2,1,0:T(8,128)}, f32[3,8,8,7168]{3,2,1,0:T(8,128)}, f32[3,8,7168]{2,1,0:T(8,128)}) custom-call(f32[3,8,8,7168]{3,2,1,0:T(8,128)S(1)} %get-tuple-element.13.fresh, f32[3,8,8,7168]{3,2,1,0:T(8,128)S(1)} %get-tuple-element.14.buddy, f32[3,8,7168]{2,1,0:T(8,128)S(1)} %get-tuple-element.15.parity), custom_call_target="tpu_custom_call" | custom-call | tf_op jit(solution)/shard_map/finish/pallas_call | solution.py:288

commit v3 on v2

--- a/solution.py
+++ b/solution.py
@@ -16,7 +16,8 @@
 XS, ZS, YS, ZLS, CORES = 4, 4, 4, 2, 2
 ZHS = ZS // ZLS
 STRIPE = 8
-LONG_STRIPES = 2
+PARTS = 4
+CUTS = 2
 F32 = jnp.float32
 DMA = pltpu.SemaphoreType.DMA
 IN_HBM = pl.BlockSpec(memory_space=pltpu.HBM)
@@ -69,23 +70,32 @@
     x_plus, x_minus = device((x + 1) % XS, y, z), device((x + XS - 1) % XS, y, z)
     z_plus, z_minus = device(x, y, (z + 1) % ZS), device(x, y, (z + ZS - 1) % ZS)
     stripes = w.shape[0]
-    short = stripes - LONG_STRIPES
     half = w.shape[2] // 2
+    part = w.shape[2] // PARTS
 
     tables = [
         pltpu.make_async_copy(owners_in, owner_ref, table_sem.at[0]),
         pltpu.make_async_copy(exponents_in, exponent_ref, table_sem.at[1]),
     ]
 
-    def loads(pair):
-        two, rows = pl.ds(2 * pair, 2), pl.ds(2 * STRIPE * pair, 2 * STRIPE)
-        ends = [(w_in.at[two], w.at[two]), (m_in.at[two], m.at[two]), (v_in.at[two], v.at[two])]
-        ends.append((g_in.at[rows], g.at[rows]))
-        return [pltpu.make_async_copy(*e, load_sem.at[pair, i]) for i, e in enumerate(ends)]
-
-    pairs = [stripes // 2 - 1, *range(stripes // 2 - 1)]
-    for pair in pairs:
-        for load in loads(pair):
+    first, last = 0, stripes // 2 - 1
+    blocks = [
+        (first, 0, part),
+        (last, 0, part),
+        (first, part, half * 2 - part),
+        (last, part, half * 2 - part),
+    ]
+    blocks += [(pair, 0, half * 2) for pair in range(first + 1, last)]
+
+    def loads(b):
+        pair, start, size = blocks[b]
+        two, rows, columns = pl.ds(2 * pair, 2), pl.ds(2 * STRIPE * pair, 2 * STRIPE), pl.ds(start, size)
+        ends = [(src.at[two, :, columns], dst.at[two, :, columns]) for src, dst in ((w_in, w), (m_in, m), (v_in, v))]
+        ends.append((g_in.at[rows, columns], g.at[rows, columns]))
+        return [pltpu.make_async_copy(*e, load_sem.at[b, i]) for i, e in enumerate(ends)]
+
+    for b in range(len(blocks)):
+        for load in loads(b):
             load.start()
 
     def send(source, target, send_sem, recv_sem, to):
@@ -99,44 +109,73 @@
         )
 
     barrier = pltpu.get_barrier_semaphore()
-    neighbours = (y_plus, y_minus, x_plus, x_minus, z_plus, z_minus)
-    for other in neighbours:
-        pl.semaphore_signal(barrier, inc=1, device_id=other, device_id_type=MESH)
+    beside, along_z = (y_plus, y_minus, x_plus, x_minus), (z_plus, z_minus)
+
+    def greet(others):
+        for other in others:
+            pl.semaphore_signal(barrier, inc=1, device_id=other, device_id_type=MESH)
+
+    greet(beside)
+
+    def meet():
+        @pl.when(zl == 0)
+        def _():
+            pl.semaphore_wait(barrier, len(beside))
+            greet(along_z)
+
+        @pl.when(zl == 1)
+        def _():
+            pl.semaphore_wait(barrier, len(beside) + len(along_z))
+            greet(along_z)
+
+    def meet_along_z():
+        @pl.when(zl == 0)
+        def _():
+            pl.semaphore_wait(barrier, len(along_z))
+
+    def update(b):
+        pair, start, size = blocks[b]
+        columns = pl.ds(start, size)
+        for load in loads(b):
+            load.wait()
+        gradient = g[pl.ds(2 * STRIPE * pair, 2 * STRIPE), columns].astype(F32)
+        for h in range(2):
+            s = 2 * pair + h
+            new = adamw(
+                w[s, :, columns], m[s, :, columns], v[s, :, columns],
+                gradient[h * STRIPE : (h + 1) * STRIPE],
+            )
+            for a in range(3):
+                fresh[a, s, :, columns] = new[a]
+
+    def plus(b):
+        pair, start, size = blocks[b]
+        here = (slice(None), pl.ds(2 * pair, 2), slice(None), pl.ds(start, size))
+        return send(fresh.at[here], buddy_ref.at[here], plus_send.at[b], plus_recv.at[b], y_plus)
+
+    def hop(step, i):
+        here = (slice(None), pl.ds(2 * last, 2), slice(None), pl.ds(i * part, part))
+        source = (fresh.at[here], hop1.at[i], hop2.at[i])[step]
+        target = (hop1.at[i], hop2.at[i], buddy_ref.at[here])[step]
+        return send(source, target, hop_send.at[step, i], hop_recv.at[step, i], y_minus)
+
+    short = [b for b in range(len(blocks)) if blocks[b][0] != last]
+
+    update(0)
+    meet()
+    plus(0).start()
     for table in tables:
         table.start()
-
-    def update(pair):
-        for load in loads(pair):
-            load.wait()
-        gradient = g[pl.ds(2 * STRIPE * pair, 2 * STRIPE), :].astype(F32)
-        for h in range(2):
-            s = 2 * pair + h
-            fresh[0, s], fresh[1, s], fresh[2, s] = adamw(
-                w[s], m[s], v[s], gradient[h * STRIPE : (h + 1) * STRIPE]
-            )
-
-    def plus(s):
-        return send(fresh.at[:, s], buddy_ref.at[:, s], plus_send.at[s], plus_recv.at[s], y_plus)
-
-    chunks = [(a, short + r) for r in range(LONG_STRIPES) for a in range(3)]
-
-    def hop(step, i):
-        a, s = chunks[i]
-        source = (fresh.at[a, s], hop1.at[i], hop2.at[i])[step]
-        target = (hop1.at[i], hop2.at[i], buddy_ref.at[a, s])[step]
-        return send(source, target, hop_send.at[step, i], hop_recv.at[step, i], y_minus)
-
-    update(pairs[0])
-    update(pairs[1])
-    pl.semaphore_wait(barrier, len(neighbours))
-    for i in range(len(chunks)):
+    update(1)
+    hop(0, 0).start()
+    update(2)
+    plus(2).start()
+    update(3)
+    for i in range(1, PARTS):
         hop(0, i).start()
-        if i < 2:
-            plus(2 * pairs[1] + i).start()
-    for pair in pairs[2:]:
-        update(pair)
-        plus(2 * pair).start()
-        plus(2 * pair + 1).start()
+    for b in short[2:]:
+        update(b)
+        plus(b).start()
 
     for table in tables:
         table.wait()
@@ -181,7 +220,7 @@
     scaled[XS + XS - 1] += first_in[1]
     sum_minus.start()
 
-    for i in range(len(chunks)):
+    for i in range(PARTS):
         hop(0, i).wait_recv()
         hop(1, i).start()
 
@@ -193,6 +232,7 @@
     out_minus = send(scaled.at[XS, :, :, right], relay.at[1], z_send.at[1], z_recv.at[1], z_minus)
     on_plus = send(relay.at[0], across.at[0], z_send.at[2], z_recv.at[2], z_plus)
     on_minus = send(relay.at[1], across.at[1], z_send.at[3], z_recv.at[3], z_minus)
+    meet_along_z()
     out_plus.start()
     out_minus.start()
     parity_ref[...] = scaled[0] + second_in[1] + second_in[2]
@@ -201,7 +241,7 @@
     out_minus.wait_recv()
     on_minus.start()
 
-    for i in range(len(chunks)):
+    for i in range(PARTS):
         hop(1, i).wait_recv()
         hop(2, i).start()
 
@@ -215,20 +255,19 @@
     for copy in (out_plus, out_minus, on_plus, on_minus):
         copy.wait_send()
     for step in range(3):
-        for i in range(len(chunks)):
+        for i in range(PARTS):
             hop(step, i).wait_send()
-    for s in range(short):
-        plus(s).wait_send()
-    for s in range(short):
-        plus(s).wait_recv()
-    for i in range(len(chunks)):
+    for b in short:
+        plus(b).wait_send()
+    for b in short:
+        plus(b).wait_recv()
+    for i in range(PARTS):
         hop(2, i).wait_recv()
 
 
 def exchange(owners, exponents, w, m, v, g):
     shape = w.shape
     stripes, _, width = shape
-    chunks = 3 * LONG_STRIPES
     block = (3, STRIPE, width)
     halves = (2, 3, STRIPE, width // 2)
     return pl.pallas_call(
@@ -252,14 +291,14 @@
             pltpu.VMEM((4, *block), F32),
             pltpu.VMEM(halves, F32),
             pltpu.VMEM(halves, F32),
-            pltpu.VMEM((chunks, STRIPE, width), F32),
-            pltpu.VMEM((chunks, STRIPE, width), F32),
-            DMA((stripes // 2, 4)),
+            pltpu.VMEM((PARTS, 3, 2, STRIPE, width // PARTS), F32),
+            pltpu.VMEM((PARTS, 3, 2, STRIPE, width // PARTS), F32),
+            DMA((stripes // 2 + 2, 4)),
             DMA((2,)),
-            DMA((stripes,)),
-            DMA((stripes,)),
-            DMA((3, chunks)),
-            DMA((3, chunks)),
+            DMA((stripes // 2 + 2,)),
+            DMA((stripes // 2 + 2,)),
+            DMA((3, PARTS)),
+            DMA((3, PARTS)),
             DMA((6,)),
             DMA((6,)),
             DMA((4,)),
@@ -273,10 +312,14 @@
 
 
 def finish_kernel(fresh, buddy, parity, w_out, m_out, v_out, buddy_out, parity_out, sem):
-    copies = [pltpu.make_async_copy(parity, parity_out, sem.at[0])]
-    for a, out in enumerate((w_out, m_out, v_out)):
-        copies.append(pltpu.make_async_copy(fresh.at[a], out, sem.at[1 + a]))
-        copies.append(pltpu.make_async_copy(buddy.at[a], buddy_out.at[a], sem.at[4 + a]))
+    copies = [pltpu.make_async_copy(parity, parity_out, sem.at[6, 0])]
+    for h in range(CUTS):
+        rows = pl.ds(h * (fresh.shape[1] // CUTS), fresh.shape[1] // CUTS)
+        for a, out in enumerate((w_out, m_out, v_out)):
+            copies.append(pltpu.make_async_copy(fresh.at[a, rows], out.at[rows], sem.at[a, h]))
+            copies.append(
+                pltpu.make_async_copy(buddy.at[a, rows], buddy_out.at[a, rows], sem.at[3 + a, h])
+            )
     for copy in copies:
         copy.start()
     for copy in copies:
@@ -296,7 +339,7 @@
         ),
         in_specs=[IN_VMEM] * 3,
         out_specs=(IN_HBM,) * 5,
-        scratch_shapes=[DMA((7,))],
+        scratch_shapes=[DMA((7, CUTS))],
         compiler_params=pltpu.CompilerParams(vmem_limit_bytes=1 << 20),
         name="finish",
     )(fresh, buddy, parity)

time: 102 us -> 102 us (level); the launches traced: 102 us -> 101 us
    pallas_call x1, Pallas kernels: 97 us -> 95.7 us  [exchange(): pl.pallas_call(exchange_kernel, out_shape=(pltpu.VMEM((3, *shape), F32),...]
where the time goes in v3:
time: 102 us; the launch traced here: 101 us
  Pallas kernels  100 us (98%)
    pallas_call x1, Pallas kernels, exchange(): pl.pallas_call(exchange_kernel, out_shape=(pltpu.VMEM((3, *shape), F32),...  95.7 us
    pallas_call x1, Pallas kernels, finish(): pl.pallas_call(finish_kernel, out_shape=(one, one, one, jax.ShapeDtypeStr...  4.41 us

profile of v3, /device:TPU:0, one launch (start us, length us, event | category | flops | bytes accessed | tf_op | source)
XLA Modules:
  0.0 100.7 jit_solution(139660885137911123)
XLA Ops:
  0.6 95.7 %exchange.1 = (f32[3,8,8,7168]{3,2,1,0:T(8,128)S(1)}, f32[3,8,8,7168]{3,2,1,0:T(8,128)S(1)}, f32[3,8,7168]{2,1,0:T(8,128)S(1)}) custom-call(s32[8,16]{1,0:T(8,128)} %bitcast.14, s32[8]{0:T(128)} %exponents_in.1, f32[8,8,7168]{2,1,0:T(8,128)} %bitcast.11, f32[8,8,7168]{2,1,0:T(8,128)} %bitcast.12, f32[8,8,7168]{2,1,0:T(8,128)} %bitcast.13, bf16[64,7168]{1,0:T(8,128)(2,1)} %g_in.1), custom_call_target="tpu_custom_call" | custom-call | tf_op jit(solution)/shard_map/exchange/pallas_call | solution.py:273
  96.3 4.4 %finish.1 = (f32[8,8,7168]{2,1,0:T(8,128)}, f32[8,8,7168]{2,1,0:T(8,128)}, f32[8,8,7168]{2,1,0:T(8,128)}, f32[3,8,8,7168]{3,2,1,0:T(8,128)}, f32[3,8,7168]{2,1,0:T(8,128)}) custom-call(f32[3,8,8,7168]{3,2,1,0:T(8,128)S(1)} %get-tuple-element.13.fresh, f32[3,8,8,7168]{3,2,1,0:T(8,128)S(1)} %get-tuple-element.14.buddy, f32[3,8,7168]{2,1,0:T(8,128)S(1)} %get-tuple-element.15.parity), custom_call_target="tpu_custom_call" | custom-call | tf_op jit(solution)/shard_map/finish/pallas_call | solution.py:331

commit v4 on v3

--- a/solution.py
+++ b/solution.py
@@ -109,29 +109,43 @@
         )
 
     barrier = pltpu.get_barrier_semaphore()
-    beside, along_z = (y_plus, y_minus, x_plus, x_minus), (z_plus, z_minus)
-
-    def greet(others):
-        for other in others:
-            pl.semaphore_signal(barrier, inc=1, device_id=other, device_id_type=MESH)
-
-    greet(beside)
+
+    def greet(other):
+        pl.semaphore_signal(barrier, inc=1, device_id=other, device_id_type=MESH)
+
+    greet(y_plus)
+    greet(y_minus)
+
+    @pl.when(x < XS - 1)
+    def _():
+        greet(x_plus)
+
+    @pl.when(x > 0)
+    def _():
+        greet(x_minus)
+
+    x_first, z_first, z_last = 1 - jnp.minimum(x, 1), 1 - jnp.minimum(z, 1), z // (ZS - 1)
 
     def meet():
-        @pl.when(zl == 0)
+        pl.semaphore_wait(barrier, 4 - x_first + 1 - z_first + z_last)
+
+        @pl.when(x == 0)
         def _():
-            pl.semaphore_wait(barrier, len(beside))
-            greet(along_z)
-
-        @pl.when(zl == 1)
+            greet(x_minus)
+
+        @pl.when(x == XS - 1)
         def _():
-            pl.semaphore_wait(barrier, len(beside) + len(along_z))
-            greet(along_z)
-
-    def meet_along_z():
-        @pl.when(zl == 0)
+            greet(x_plus)
+
+        greet(z_plus)
+        greet(z_minus)
+
+    def meet_the_rest():
+        rest = x_first + z_first + 1 - z_last
+
+        @pl.when(rest > 0)
         def _():
-            pl.semaphore_wait(barrier, len(along_z))
+            pl.semaphore_wait(barrier, rest)
 
     def update(b):
         pair, start, size = blocks[b]
@@ -180,6 +194,7 @@
     for table in tables:
         table.wait()
     exponent = exponent_ref[group]
+    meet_the_rest()
 
     def scale(dx, dz):
         owner = ((zh + dz) % ZHS) * XS + (x + dx) % XS
@@ -232,7 +247,6 @@
     out_minus = send(scaled.at[XS, :, :, right], relay.at[1], z_send.at[1], z_recv.at[1], z_minus)
     on_plus = send(relay.at[0], across.at[0], z_send.at[2], z_recv.at[2], z_plus)
     on_minus = send(relay.at[1], across.at[1], z_send.at[3], z_recv.at[3], z_minus)
-    meet_along_z()
     out_plus.start()
     out_minus.start()
     parity_ref[...] = scaled[0] + second_in[1] + second_in[2]

time: 102 us -> 99.8 us (0.978)
  Pallas kernels: 100 us -> 98.8 us
    pallas_call x1, Pallas kernels: 95.7 us -> 94.4 us  [exchange(): pl.pallas_call(exchange_kernel, out_shape=(pltpu.VMEM((3, *shape), F32),...]
where the time goes in v4:
time: 99.8 us; the launch traced here: 99.5 us
  Pallas kernels  98.8 us (99%)
    pallas_call x1, Pallas kernels, exchange(): pl.pallas_call(exchange_kernel, out_shape=(pltpu.VMEM((3, *shape), F32),...  94.4 us
    pallas_call x1, Pallas kernels, finish(): pl.pallas_call(finish_kernel, out_shape=(one, one, one, jax.ShapeDtypeStr...  4.41 us

profile of v4, /device:TPU:0, one launch (start us, length us, event | category | flops | bytes accessed | tf_op | source)
XLA Modules:
  0.0 99.5 jit_solution(9320530002372441739)
XLA Ops:
  0.6 94.4 %exchange.1 = (f32[3,8,8,7168]{3,2,1,0:T(8,128)S(1)}, f32[3,8,8,7168]{3,2,1,0:T(8,128)S(1)}, f32[3,8,7168]{2,1,0:T(8,128)S(1)}) custom-call(s32[8,16]{1,0:T(8,128)} %bitcast.14, s32[8]{0:T(128)} %exponents_in.1, f32[8,8,7168]{2,1,0:T(8,128)} %bitcast.11, f32[8,8,7168]{2,1,0:T(8,128)} %bitcast.12, f32[8,8,7168]{2,1,0:T(8,128)} %bitcast.13, bf16[64,7168]{1,0:T(8,128)(2,1)} %g_in.1), custom_call_target="tpu_custom_call" | custom-call | tf_op jit(solution)/shard_map/exchange/pallas_call | solution.py:287
  95.1 4.4 %finish.1 = (f32[8,8,7168]{2,1,0:T(8,128)}, f32[8,8,7168]{2,1,0:T(8,128)}, f32[8,8,7168]{2,1,0:T(8,128)}, f32[3,8,8,7168]{3,2,1,0:T(8,128)}, f32[3,8,7168]{2,1,0:T(8,128)}) custom-call(f32[3,8,8,7168]{3,2,1,0:T(8,128)S(1)} %get-tuple-element.13.fresh, f32[3,8,8,7168]{3,2,1,0:T(8,128)S(1)} %get-tuple-element.14.buddy, f32[3,8,7168]{2,1,0:T(8,128)S(1)} %get-tuple-element.15.parity), custom_call_target="tpu_custom_call" | custom-call | tf_op jit(solution)/shard_map/finish/pallas_call | solution.py:345

commit v5 on v3

--- a/solution.py
+++ b/solution.py
@@ -16,7 +16,8 @@
 XS, ZS, YS, ZLS, CORES = 4, 4, 4, 2, 2
 ZHS = ZS // ZLS
 STRIPE = 8
-PARTS = 4
+PARTS = (512, 2048, 2176, 2304)
+EXTRA = 128
 CUTS = 2
 F32 = jnp.float32
 DMA = pltpu.SemaphoreType.DMA
@@ -30,10 +31,10 @@
     second = beta_two * moment2 + (1.0 - beta_two) * grad_float * grad_float
     correct_one = 1.0 - beta_one**step_count
     correct_two = 1.0 - beta_two**step_count
-    update = (
-        first / correct_one / (jnp.sqrt(second / correct_two) + epsilon) + weight_decay * weight
-    )
-    return (weight - learning_rate * update, first, second)
+    scaled_second = second * (1.0 / correct_two)
+    spread = scaled_second * lax.rsqrt(scaled_second) + epsilon
+    step = first * (learning_rate / correct_one) / spread
+    return (weight * (1.0 - learning_rate * weight_decay) - step, first, second)
 
 
 def coefficient(stripe, exponent):
@@ -54,8 +55,8 @@
 
 def exchange_kernel(
     owners_in, exponents_in, w_in, m_in, v_in, g_in, fresh, buddy_ref, parity_ref,
-    w, m, v, g, owner_ref, exponent_ref, scaled, first_in, second_in, relay, across, hop1, hop2,
-    load_sem, table_sem, plus_send, plus_recv, hop_send, hop_recv, x_send, x_recv, z_send, z_recv,
+    w, m, v, g, owner_ref, exponent_ref, scaled, first_in, second_in, relay, across, hop1, hop2, extra1, extra2,
+    load_sem, table_sem, plus_send, plus_recv, hop_send, hop_recv, x_send, x_recv, z_send, z_recv, ring_sem,
 ):
     group = lax.axis_index("group")
     domain = lax.axis_index("domain")
@@ -71,7 +72,8 @@
     z_plus, z_minus = device(x, y, (z + 1) % ZS), device(x, y, (z + ZS - 1) % ZS)
     stripes = w.shape[0]
     half = w.shape[2] // 2
-    part = w.shape[2] // PARTS
+    width = w.shape[2]
+    short_width = width - EXTRA
 
     tables = [
         pltpu.make_async_copy(owners_in, owner_ref, table_sem.at[0]),
@@ -80,12 +82,12 @@
 
     first, last = 0, stripes // 2 - 1
     blocks = [
-        (first, 0, part),
-        (last, 0, part),
-        (first, part, half * 2 - part),
-        (last, part, half * 2 - part),
+        (first, 0, PARTS[0]),
+        (last, 0, PARTS[0]),
+        (first, PARTS[0], width - PARTS[0]),
+        (last, PARTS[0], width - PARTS[0]),
     ]
-    blocks += [(pair, 0, half * 2) for pair in range(first + 1, last)]
+    blocks += [(pair, 0, width) for pair in range(first + 1, last)]
 
     def loads(b):
         pair, start, size = blocks[b]
@@ -109,29 +111,66 @@
         )
 
     barrier = pltpu.get_barrier_semaphore()
-    beside, along_z = (y_plus, y_minus, x_plus, x_minus), (z_plus, z_minus)
-
-    def greet(others):
+
+    def greet(*others, semaphore=barrier):
         for other in others:
-            pl.semaphore_signal(barrier, inc=1, device_id=other, device_id_type=MESH)
-
-    greet(beside)
+            pl.semaphore_signal(semaphore, inc=1, device_id=other, device_id_type=MESH)
+
+    greet(y_plus, y_minus)
+
+    @pl.when(y == 0)
+    def _():
+        greet(x_plus, x_minus)
+
+        @pl.when(z < ZS - 1)
+        def _():
+            greet(z_plus)
+
+        @pl.when(z > 0)
+        def _():
+            greet(z_minus)
 
     def meet():
-        @pl.when(zl == 0)
-        def _():
-            pl.semaphore_wait(barrier, len(beside))
-            greet(along_z)
-
-        @pl.when(zl == 1)
-        def _():
-            pl.semaphore_wait(barrier, len(beside) + len(along_z))
-            greet(along_z)
-
-    def meet_along_z():
-        @pl.when(zl == 0)
-        def _():
-            pl.semaphore_wait(barrier, len(along_z))
+        @pl.when(y > 0)
+        def _():
+            pl.semaphore_wait(barrier, 2)
+
+        @pl.when((y == 0) & (z == 0))
+        def _():
+            pl.semaphore_wait(barrier, 5)
+            greet(z_minus)
+
+        @pl.when((y == 0) & (z > 0))
+        def _():
+            pl.semaphore_wait(barrier, 6)
+
+        @pl.when((y == 0) & (z == ZS - 1))
+        def _():
+            greet(z_plus)
+
+        @pl.when(y == 1)
+        def _():
+            greet(y_minus, semaphore=ring_sem.at[0])
+
+    def meet_the_rest():
+        @pl.when((y == 0) & (z == 0))
+        def _():
+            pl.semaphore_wait(barrier, 1)
+
+        @pl.when(y == 0)
+        def _():
+            pl.semaphore_wait(ring_sem.at[0], 1)
+            greet(x_plus, x_minus, z_plus, z_minus, semaphore=ring_sem.at[1])
+            pl.semaphore_wait(ring_sem.at[1], 4)
+            greet(y_plus, y_minus, semaphore=ring_sem.at[2])
+
+        @pl.when(y > 0)
+        def _():
+            pl.semaphore_wait(ring_sem.at[2], 1)
+
+        @pl.when(y == 1)
+        def _():
+            greet(y_plus, semaphore=ring_sem.at[2])
 
     def update(b):
         pair, start, size = blocks[b]
@@ -150,14 +189,47 @@
 
     def plus(b):
         pair, start, size = blocks[b]
+        if pair == last - 1:
+            size = short_width - start
         here = (slice(None), pl.ds(2 * pair, 2), slice(None), pl.ds(start, size))
         return send(fresh.at[here], buddy_ref.at[here], plus_send.at[b], plus_recv.at[b], y_plus)
 
     def hop(step, i):
-        here = (slice(None), pl.ds(2 * last, 2), slice(None), pl.ds(i * part, part))
-        source = (fresh.at[here], hop1.at[i], hop2.at[i])[step]
-        target = (hop1.at[i], hop2.at[i], buddy_ref.at[here])[step]
+        start, size = sum(PARTS[:i]), PARTS[i]
+        here = (slice(None), pl.ds(2 * last, 2), slice(None), pl.ds(start, size))
+        held = (i, slice(None), slice(None), slice(None), pl.ds(0, size))
+        source = (fresh.at[here], hop1.at[held], hop2.at[held])[step]
+        target = (hop1.at[held], hop2.at[held], buddy_ref.at[here])[step]
         return send(source, target, hop_send.at[step, i], hop_recv.at[step, i], y_minus)
+
+    left_over = (slice(None), pl.ds(2 * last - 2, 4), slice(None), pl.ds(short_width, EXTRA))
+
+    def plus_extra():
+        here = (fresh.at[left_over], buddy_ref.at[left_over])
+        return send(*here, plus_send.at[1], plus_recv.at[1], y_plus)
+
+    def hop_extra(step):
+        source = (fresh.at[left_over], extra1, extra2)[step]
+        target = (extra1, extra2, buddy_ref.at[left_over])[step]
+        return send(source, target, hop_send.at[step, len(PARTS)], hop_recv.at[step, len(PARTS)], y_minus)
+
+    def by_start(behind, act_long, act_short):
+        goes_long = ((y + behind + 1) % YS) // 2 == 0
+        if act_long is not None:
+            pl.when(goes_long)(act_long)
+        if act_short is not None:
+            pl.when(jnp.logical_not(goes_long))(act_short)
+
+    def pass_on(step):
+        for i in range(len(PARTS)):
+            hop(step, i).wait_recv()
+            hop(step + 1, i).start()
+
+        def extra():
+            hop_extra(step).wait_recv()
+            hop_extra(step + 1).start()
+
+        by_start(step + 1, extra, None)
 
     short = [b for b in range(len(blocks)) if blocks[b][0] != last]
 
@@ -171,15 +243,17 @@
     update(2)
     plus(2).start()
     update(3)
-    for i in range(1, PARTS):
+    for i in range(1, len(PARTS)):
         hop(0, i).start()
     for b in short[2:]:
         update(b)
         plus(b).start()
+    by_start(0, lambda: hop_extra(0).start(), lambda: plus_extra().start())
 
     for table in tables:
         table.wait()
     exponent = exponent_ref[group]
+    meet_the_rest()
 
     def scale(dx, dz):
         owner = ((zh + dz) % ZHS) * XS + (x + dx) % XS
@@ -220,9 +294,7 @@
     scaled[XS + XS - 1] += first_in[1]
     sum_minus.start()
 
-    for i in range(PARTS):
-        hop(0, i).wait_recv()
-        hop(1, i).start()
+    pass_on(0)
 
     for copy in (near_plus, near_minus, sum_plus, sum_minus):
         copy.wait_recv()
@@ -232,19 +304,16 @@
     out_minus = send(scaled.at[XS, :, :, right], relay.at[1], z_send.at[1], z_recv.at[1], z_minus)
     on_plus = send(relay.at[0], across.at[0], z_send.at[2], z_recv.at[2], z_plus)
     on_minus = send(relay.at[1], across.at[1], z_send.at[3], z_recv.at[3], z_minus)
-    meet_along_z()
     out_plus.start()
     out_minus.start()
     parity_ref[...] = scaled[0] + second_in[1] + second_in[2]
+
+    pass_on(1)
+
     out_plus.wait_recv()
     on_plus.start()
     out_minus.wait_recv()
     on_minus.start()
-
-    for i in range(PARTS):
-        hop(1, i).wait_recv()
-        hop(2, i).start()
-
     on_plus.wait_recv()
     parity_ref[:, :, left] += across[0]
     on_minus.wait_recv()
@@ -255,14 +324,18 @@
     for copy in (out_plus, out_minus, on_plus, on_minus):
         copy.wait_send()
     for step in range(3):
-        for i in range(PARTS):
+        for i in range(len(PARTS)):
             hop(step, i).wait_send()
+        by_start(step, lambda: hop_extra(step).wait_send(), None)
+    by_start(0, None, lambda: plus_extra().wait_send())
     for b in short:
         plus(b).wait_send()
+    by_start(YS - 1, None, lambda: plus_extra().wait_recv())
     for b in short:
         plus(b).wait_recv()
-    for i in range(PARTS):
+    for i in range(len(PARTS)):
         hop(2, i).wait_recv()
+    by_start(YS - 1, lambda: hop_extra(2).wait_recv(), None)
 
 
 def exchange(owners, exponents, w, m, v, g):
@@ -291,18 +364,21 @@
             pltpu.VMEM((4, *block), F32),
             pltpu.VMEM(halves, F32),
             pltpu.VMEM(halves, F32),
-            pltpu.VMEM((PARTS, 3, 2, STRIPE, width // PARTS), F32),
-            pltpu.VMEM((PARTS, 3, 2, STRIPE, width // PARTS), F32),
+            pltpu.VMEM((len(PARTS), 3, 2, STRIPE, max(PARTS)), F32),
+            pltpu.VMEM((len(PARTS), 3, 2, STRIPE, max(PARTS)), F32),
+            pltpu.VMEM((3, 4, STRIPE, EXTRA), F32),
+            pltpu.VMEM((3, 4, STRIPE, EXTRA), F32),
             DMA((stripes // 2 + 2, 4)),
             DMA((2,)),
             DMA((stripes // 2 + 2,)),
             DMA((stripes // 2 + 2,)),
-            DMA((3, PARTS)),
-            DMA((3, PARTS)),
+            DMA((3, len(PARTS) + 1)),
+            DMA((3, len(PARTS) + 1)),
             DMA((6,)),
             DMA((6,)),
             DMA((4,)),
             DMA((4,)),
+            pltpu.SemaphoreType.REGULAR((3,)),
         ],
         compiler_params=pltpu.CompilerParams(
             collective_id=0, has_side_effects=True, vmem_limit_bytes=40 << 20

time: 102 us -> 98.9 us (0.970)
  Pallas kernels: 100 us -> 97.9 us
    pallas_call x1, Pallas kernels: 95.7 us -> 93.5 us  [exchange(): pl.pallas_call(exchange_kernel, out_shape=(pltpu.VMEM((3, *shape), F32),...]
where the time goes in v5:
time: 98.9 us; the launch traced here: 98.6 us
  Pallas kernels  97.9 us (99%)
    pallas_call x1, Pallas kernels, exchange(): pl.pallas_call(exchange_kernel, out_shape=(pltpu.VMEM((3, *shape), F32),...  93.5 us
    pallas_call x1, Pallas kernels, finish(): pl.pallas_call(finish_kernel, out_shape=(one, one, one, jax.ShapeDtypeStr...  4.41 us

profile of v5, /device:TPU:0, one launch (start us, length us, event | category | flops | bytes accessed | tf_op | source)
XLA Modules:
  0.0 98.6 jit_solution(16521960381981736694)
XLA Ops:
  0.6 93.5 %exchange.1 = (f32[3,8,8,7168]{3,2,1,0:T(8,128)S(1)}, f32[3,8,8,7168]{3,2,1,0:T(8,128)S(1)}, f32[3,8,7168]{2,1,0:T(8,128)S(1)}) custom-call(s32[8,16]{1,0:T(8,128)} %bitcast.14, s32[8]{0:T(128)} %exponents_in.1, f32[8,8,7168]{2,1,0:T(8,128)} %bitcast.11, f32[8,8,7168]{2,1,0:T(8,128)} %bitcast.12, f32[8,8,7168]{2,1,0:T(8,128)} %bitcast.13, bf16[64,7168]{1,0:T(8,128)(2,1)} %g_in.1), custom_call_target="tpu_custom_call" | custom-call | tf_op jit(solution)/shard_map/exchange/pallas_call | solution.py:346
  94.2 4.4 %finish.1 = (f32[8,8,7168]{2,1,0:T(8,128)}, f32[8,8,7168]{2,1,0:T(8,128)}, f32[8,8,7168]{2,1,0:T(8,128)}, f32[3,8,8,7168]{3,2,1,0:T(8,128)}, f32[3,8,7168]{2,1,0:T(8,128)}) custom-call(f32[3,8,8,7168]{3,2,1,0:T(8,128)S(1)} %get-tuple-element.13.fresh, f32[3,8,8,7168]{3,2,1,0:T(8,128)S(1)} %get-tuple-element.14.buddy, f32[3,8,7168]{2,1,0:T(8,128)S(1)} %get-tuple-element.15.parity), custom_call_target="tpu_custom_call" | custom-call | tf_op jit(solution)/shard_map/finish/pallas_call | solution.py:407

commit v6 on v0

v6 whole, which is shorter than its diff:
```python
import jax
import jax.numpy as jnp
from jax import lax
from jax.experimental import pallas as pl
from jax.experimental.pallas import tpu as pltpu
from jax.sharding import PartitionSpec as P

beta_one = 0.9
beta_two = 0.95
learning_rate = 0.02
weight_decay = 0.1
epsilon = 1e-08
step_count = 100.0

MESH = pl.DeviceIdType.MESH
XS, ZS, YS, ZLS, CORES = 4, 4, 4, 2, 2
ZHS = ZS // ZLS
STRIPE = 8
LONG = (
    (((0, 512), (512, 1536), (2048, 1536)), ((3584, 1152), (4736, 1152), (5888, 1280))),
    (((0, 512), (512, 2304), (2816, 2304)), ((5120, 1024), (6144, 1024))),
)
SHORT = (
    (((0, 0, 512), (0, 512, 6656), (1, 0, 3584)), ((1, 3584, 3584), (2, 0, 7168))),
    (((0, 0, 512), (0, 512, 6656), (1, 0, 7168), (2, 0, 1024)), ((2, 1024, 6144),)),
)
F32 = jnp.float32
DMA = pltpu.SemaphoreType.DMA
IN_HBM = pl.BlockSpec(memory_space=pltpu.HBM)
IN_VMEM = pl.BlockSpec(memory_space=pltpu.VMEM)


def adamw(weight, moment1, moment2, gradient):
    grad_float = gradient.astype(F32)
    first = beta_one * moment1 + (1.0 - beta_one) * grad_float
    second = beta_two * moment2 + (1.0 - beta_two) * grad_float * grad_float
    correct_one = 1.0 - beta_one**step_count
    correct_two = 1.0 - beta_two**step_count
    scaled_second = second * (1.0 / correct_two)
    spread = scaled_second * lax.rsqrt(scaled_second) + epsilon
    step = first * (learning_rate / correct_one) / spread
    return (weight * (1.0 - learning_rate * weight_decay) - step, first, second)


def coefficient(stripe, exponent):
    bits = [(jnp.right_shift(exponent, i) & 1).astype(F32) for i in range(3)]
    point = 1.0 + (2.0 * stripe.astype(F32) - 7.0) / 32.0
    square = point * point
    fourth = square * square
    power = 1.0
    for bit, factor in zip(bits, (point, square, fourth)):
        power = power * (1.0 + bit * (factor - 1.0))
    return power


def same(a, b):
    gap = a - b
    return 1 - jnp.minimum(jnp.maximum(gap, -gap), 1)


def loading_kernel(
    owners_in, exponents_in, w_in, m_in, v_in, g_in, fresh, buddy_ref, part_ref, cross_ref,
    w, m, v, g, load_sem, *rest,
):
    last, width = w.shape[0] // 2 - 1, w.shape[2]
    cut = LONG[0][0][0][1]
    blocks = [(0, 0, cut), (last, 0, cut), (0, cut, width - cut), (last, cut, width - cut)]
    blocks += [(pair, 0, width) for pair in range(1, last)]

    def loads(b):
        pair, start, size = blocks[b]
        two, rows, columns = pl.ds(2 * pair, 2), pl.ds(2 * STRIPE * pair, 2 * STRIPE), pl.ds(start, size)
        ends = [(src.at[two, :, columns], dst.at[two, :, columns]) for src, dst in ((w_in, w), (m_in, m), (v_in, v))]
        ends.append((g_in.at[rows, columns], g.at[rows, columns]))
        return [pltpu.make_async_copy(*e, load_sem.at[b, i]) for i, e in enumerate(ends)]

    def update(b):
        pair, start, size = blocks[b]
        columns = pl.ds(start, size)
        for load in loads(b):
            load.wait()
        gradient = g[pl.ds(2 * STRIPE * pair, 2 * STRIPE), columns].astype(F32)
        for h in range(2):
            s = 2 * pair + h
            new = adamw(
                w[s, :, columns], m[s, :, columns], v[s, :, columns],
                gradient[h * STRIPE : (h + 1) * STRIPE],
            )
            for a in range(3):
                fresh[a, s, :, columns] = new[a]

    def start_loads():
        for b in range(len(blocks)):
            for load in loads(b):
                load.start()

    arrays = (fresh, buddy_ref, part_ref, cross_ref)
    exchange_kernel(0, arrays, rest, (start_loads, update, owners_in, exponents_in))


def second_kernel(fresh, after, part_ref, cross_ref, buddy_ref, parity_ref, *rest):
    exchange_kernel(1, (fresh, buddy_ref, part_ref, cross_ref), rest, parity_ref)


def exchange_kernel(phase, arrays, scratch, more):
    fresh, buddy_ref, part_ref, cross_ref = arrays
    hop1, hop2, plus_send, plus_recv, hop_send, hop_recv, ring_sem = scratch[:7]
    if phase == 0:
        start_loads, update, owners_in, exponents_in = more
        owner_ref, exponent_ref, scaled, first_in, second_in, table_sem, x_send, x_recv = scratch[7:]
    else:
        parity_ref = more
        relay, across, z_send, z_recv = scratch[7:]
    group = lax.axis_index("group")
    domain = lax.axis_index("domain")
    x, zh = group % XS, group // XS
    core, zl, y = domain % CORES, (domain // CORES) % ZLS, domain // (CORES * ZLS)
    z = zh * ZLS + zl

    def device(x, y, z):
        return ((z // ZLS) * XS + x, (y * ZLS + z % ZLS) * CORES + core)

    y_plus, y_minus = device(x, (y + 1) % YS, z), device(x, (y + YS - 1) % YS, z)
    x_plus, x_minus = device((x + 1) % XS, y, z), device((x + XS - 1) % XS, y, z)
    z_plus, z_minus = device(x, y, (z + 1) % ZS), device(x, y, (z + ZS - 1) % ZS)
    stripes = fresh.shape[1]
    half = fresh.shape[3] // 2
    last = stripes // 2 - 1

    if phase == 0:
        start_loads()

    def send(source, target, send_sem, recv_sem, to):
        return pltpu.make_async_remote_copy(
            src_ref=source,
            dst_ref=target,
            send_sem=send_sem,
            recv_sem=recv_sem,
            device_id=to,
            device_id_type=MESH,
        )

    barrier = pltpu.get_barrier_semaphore()

    def greet(*others, semaphore=barrier):
        for other in others:
            pl.semaphore_signal(semaphore, inc=1, device_id=other, device_id_type=MESH)

    greet(y_plus, y_minus)

    corner = y == 0

    @pl.when(corner)
    def _():
        greet(x_plus, x_minus)

        @pl.when(z < ZS - 1)
        def _():
            greet(z_plus)

        @pl.when(z > 0)
        def _():
            greet(z_minus)

    if phase == 0:
        update(0)

    @pl.when(jnp.logical_not(corner))
    def _():
        pl.semaphore_wait(barrier, 2)

    @pl.when(corner & (z == 0))
    def _():
        pl.semaphore_wait(barrier, 5)
        greet(z_minus)

    @pl.when(corner & (z > 0))
    def _():
        pl.semaphore_wait(barrier, 6)

    @pl.when(corner & (z == ZS - 1))
    def _():
        greet(z_plus)

    @pl.when(y == 1)
    def _():
        greet(y_minus, semaphore=ring_sem.at[0])

    def meet_the_rest():
        @pl.when((y == 0) & (z == 0))
        def _():
            pl.semaphore_wait(barrier, 1)

        @pl.when(y == 0)
        def _():
            pl.semaphore_wait(ring_sem.at[0], 1)
            greet(x_plus, x_minus, z_plus, z_minus, semaphore=ring_sem.at[1])
            pl.semaphore_wait(ring_sem.at[1], 4)
            greet(y_plus, y_minus, semaphore=ring_sem.at[2])

        @pl.when(y > 0)
        def _():
            pl.semaphore_wait(ring_sem.at[2], 1)

        @pl.when(y == 1)
        def _():
            greet(y_plus, semaphore=ring_sem.at[2])

    def short(c):
        copies = []
        for i, (pair, start, size) in enumerate(SHORT[c][phase]):
            here = (slice(None), pl.ds(2 * pair, 2), slice(None), pl.ds(start, size))
            copies.append(send(fresh.at[here], buddy_ref.at[here], plus_send.at[i], plus_recv.at[i], y_plus))
        return copies

    def hops(c, step):
        copies = []
        for i, (start, size) in enumerate(LONG[c][phase]):
            here = (slice(None), pl.ds(2 * last, 2), slice(None), pl.ds(start, size))
            held = (i, slice(None), slice(None), slice(None), pl.ds(0, size))
            source = (fresh.at[here], hop1.at[held], hop2.at[held])[step]
            target = (hop1.at[held], hop2.at[held], buddy_ref.at[here])[step]
            copies.append(send(source, target, hop_send.at[step, i], hop_recv.at[step, i], y_minus))
        return copies

    def by_core(act):
        for c in range(CORES):
            pl.when(core == c)(lambda c=c: act(c))

    def start_all(copies):
        for copy in copies:
            copy.start()

    def pass_on(c, step, chunks=slice(None)):
        for arrived, on in list(zip(hops(c, step), hops(c, step + 1)))[chunks]:
            arrived.wait_recv()
            on.start()

    def end(c):
        for step in range(3):
            for copy in hops(c, step):
                copy.wait_send()
        for copy in short(c):
            copy.wait()
        for copy in hops(c, 2):
            copy.wait_recv()

    if phase == 1:
        left, right = pl.ds(0, half), pl.ds(half, half)
        out_plus = send(cross_ref.at[:, :, left], relay.at[0], z_send.at[0], z_recv.at[0], z_plus)
        out_minus = send(cross_ref.at[:, :, right], relay.at[1], z_send.at[1], z_recv.at[1], z_minus)
        on_plus = send(relay.at[0], across.at[0], z_send.at[2], z_recv.at[2], z_plus)
        on_minus = send(relay.at[1], across.at[1], z_send.at[3], z_recv.at[3], z_minus)

        def totals():
            out_plus.wait_recv()
            on_plus.start()
            out_minus.wait_recv()
            on_minus.start()
            on_plus.wait_recv()
            parity_ref[:, :, left] = part_ref[:, :, left] + across[0]
            on_minus.wait_recv()
            parity_ref[:, :, right] = part_ref[:, :, right] + across[1]
            for copy in (out_plus, out_minus, on_plus, on_minus):
                copy.wait_send()

        def all_of(c):
            start_all(hops(c, 0) + short(c))
            meet_the_rest()
            out_plus.start()
            out_minus.start()
            pass_on(c, 0)
            pass_on(c, 1)
            totals()
            end(c)

        by_core(all_of)
        return

    tables = [
        pltpu.make_async_copy(owners_in, owner_ref, table_sem.at[0]),
        pltpu.make_async_copy(exponents_in, exponent_ref, table_sem.at[1]),
    ]
    by_core(lambda c: short(c)[0].start())
    start_all(tables)
    update(1)
    by_core(lambda c: hops(c, 0)[0].start())
    update(2)
    by_core(lambda c: short(c)[1].start())
    update(3)
    by_core(lambda c: start_all(hops(c, 0)[1:]))
    update(4)
    by_core(lambda c: short(c)[2].start())
    update(5)
    by_core(lambda c: start_all(short(c)[3:]))
    for table in tables:
        table.wait()
    meet_the_rest()

    def scale(dx, dz):
        owner = ((zh + dz) % ZHS) * XS + (x + dx) % XS
        stripe = jnp.int32(0)
        for s in range(stripes):
            stripe = stripe + s * same(owner_ref[s, domain], owner)
        stripe = jnp.minimum(stripe, stripes - 1)
        factor = coefficient(stripe, exponent_ref[group])
        for a in range(3):
            scaled[dz * XS + dx, a] = fresh[a, stripe] * factor

    def along_x(i, slot, target, to):
        return send(scaled.at[slot], target, x_send.at[i], x_recv.at[i], to)

    far_plus = along_x(0, 2, first_in.at[0], x_plus)
    far_minus = along_x(1, XS + 2, first_in.at[1], x_minus)
    near_plus = along_x(2, XS + 1, second_in.at[0], x_plus)
    near_minus = along_x(3, XS - 1, second_in.at[1], x_minus)
    sum_plus = along_x(4, 1, second_in.at[2], x_plus)
    sum_minus = along_x(5, XS + XS - 1, second_in.at[3], x_minus)
    def terms():
        scale(2, 0)
        far_plus.start()
        scale(2, 1)
        far_minus.start()
        scale(1, 1)
        near_plus.start()
        scale(3, 0)
        near_minus.start()
        scale(1, 0)
        scale(3, 1)
        scale(0, 0)
        scale(0, 1)

    def first_sums():
        far_plus.wait_recv()
        scaled[1] += first_in[0]
        sum_plus.start()
        far_minus.wait_recv()
        scaled[XS + XS - 1] += first_in[1]
        sum_minus.start()

    def sums():
        for copy in (near_plus, near_minus, sum_plus, sum_minus):
            copy.wait_recv()
        cross_ref[...] = scaled[XS] + second_in[0] + second_in[3]
        part_ref[...] = scaled[0] + second_in[1] + second_in[2]
        for copy in (far_plus, far_minus, near_plus, near_minus, sum_plus, sum_minus):
            copy.wait_send()

    @pl.when(core == 0)
    def _():
        terms()
        pass_on(0, 0)
        first_sums()
        pass_on(0, 1)
        sums()
        end(0)

    @pl.when(core == 1)
    def _():
        pass_on(1, 0)
        terms()
        pass_on(1, 1, slice(0, 2))
        first_sums()
        pass_on(1, 1, slice(2, None))
        sums()
        end(1)


def exchange(phase, shape, *arrays):
    stripes, _, width = shape
    block = (3, STRIPE, width)
    halves = (2, 3, STRIPE, width // 2)
    most_long = max(len(core[phase]) for core in LONG)
    most_short = max(len(core[phase]) for core in SHORT)
    held = (most_long, 3, 2, STRIPE, max(size for core in LONG for _, size in core[phase]))
    whole = pltpu.VMEM((3, *shape), F32)
    scratch = [pltpu.VMEM(held, F32)] * 2 + [DMA((most_short,))] * 2 + [DMA((3, most_long))] * 2
    scratch += [pltpu.SemaphoreType.REGULAR((3,))]
    if phase == 0:
        gradient = arrays[5]
        loaded = [pltpu.VMEM(shape, F32)] * 3 + [pltpu.VMEM(gradient.shape, gradient.dtype)]
        scratch = [*loaded, DMA((stripes // 2 + 2, 4)), *scratch]
        scratch += [
            pltpu.SMEM(arrays[0].shape, jnp.int32),
            pltpu.SMEM(arrays[1].shape, jnp.int32),
            pltpu.VMEM((XS * ZHS, *block), F32),
            pltpu.VMEM((2, *block), F32),
            pltpu.VMEM((4, *block), F32),
            DMA((2,)),
            DMA((6,)),
            DMA((6,)),
        ]
    else:
        scratch += [pltpu.VMEM(halves, F32)] * 2 + [DMA((4,))] * 2
    part = pltpu.VMEM(block, F32)
    return pl.pallas_call(
        (loading_kernel, second_kernel)[phase],
        out_shape=((whole, whole, part, part), (whole, part))[phase],
        in_specs=([IN_HBM] * 6, [IN_VMEM] * 4)[phase],
        out_specs=(IN_VMEM,) * (4, 2)[phase],
        scratch_shapes=scratch,
        compiler_params=pltpu.CompilerParams(
            collective_id=phase, has_side_effects=True, vmem_limit_bytes=(34 << 20, 16 << 20)[phase]
        ),
        name=("exchange_one", "exchange_two")[phase],
    )(*arrays)


def places(phase, source, target, sem):
    for c in range(CORES):
        rectangles = [(2 * pair, start, size) for pair, start, size in SHORT[c][phase]]
        rectangles += [(source.shape[1] - 2, start, size) for start, size in LONG[c][phase]]
        copies = []
        for i, (s, start, size) in enumerate(rectangles):
            here = (slice(None), pl.ds(s, 2), slice(None), pl.ds(start, size))
            copies.append(pltpu.make_async_copy(source.at[here], target.at[here], sem.at[i]))
        yield c, copies


def run_by_core(groups, others):
    core = lax.axis_index("domain") % CORES

    def all_of(copies):
        for copy in copies:
            copy.start()
        for copy in copies:
            copy.wait()

    for c, copies in groups:
        pl.when(core == c)(lambda c=c, copies=copies: all_of(others + copies))


MOST = max(len(SHORT[c][p]) + len(LONG[c][p]) for c in range(CORES) for p in range(2))


def middle_kernel(fresh, buddy, w_out, m_out, v_out, buddy_out, mark, sem, other_sem):
    mark[...] = jnp.zeros(mark.shape, F32)
    outs = enumerate((w_out, m_out, v_out))
    copies = [pltpu.make_async_copy(fresh.at[a], out, other_sem.at[a]) for a, out in outs]
    run_by_core(places(0, buddy, buddy_out, sem), copies)


def middle(fresh, buddy):
    one = jax.ShapeDtypeStruct(fresh.shape[1:], F32)
    return pl.pallas_call(
        middle_kernel,
        out_shape=(one, one, one, jax.ShapeDtypeStruct(buddy.shape, F32), pltpu.VMEM((STRIPE, 128), F32)),
        in_specs=[IN_VMEM] * 2,
        out_specs=(IN_HBM,) * 4 + (IN_VMEM,),
        scratch_shapes=[DMA((MOST,)), DMA((3,))],
        compiler_params=pltpu.CompilerParams(vmem_limit_bytes=1 << 20),
        name="middle",
    )(fresh, buddy)


def finish_kernel(buddy, parity, buddy_in, buddy_out, parity_out, sem, other_sem):
    copies = [pltpu.make_async_copy(parity, parity_out, other_sem.at[0])]
    run_by_core(places(1, buddy, buddy_out, sem), copies)


def finish(buddy, parity, buddy_out):
    return pl.pallas_call(
        finish_kernel,
        out_shape=(
            jax.ShapeDtypeStruct(buddy.shape, F32),
            jax.ShapeDtypeStruct(parity.shape, F32),
        ),
        in_specs=[IN_VMEM] * 2 + [IN_HBM],
        out_specs=(IN_HBM,) * 2,
        input_output_aliases={2: 0},
        scratch_shapes=[DMA((MOST,)), DMA((1,))],
        compiler_params=pltpu.CompilerParams(vmem_limit_bytes=1 << 20),
        name="finish",
    )(buddy, parity, buddy_out)


def shards(weight, moment1, moment2, gradient, owner_table, exponents):
    rows, width = weight.shape
    w, m, v = (a.reshape(rows // STRIPE, STRIPE, width) for a in (weight, moment1, moment2))
    held = (owner_table.T, exponents, w, m, v, gradient)
    held = [pltpu.with_memory_space_constraint(a, pltpu.HBM) for a in held]
    shape = w.shape
    fresh, buddy, part, cross = exchange(0, shape, *held)
    w, m, v, buddy_out, mark = middle(fresh, buddy)
    buddy, parity = exchange(1, shape, fresh, mark, part, cross)
    buddy, parity = finish(buddy, parity, buddy_out)
    buddy = jnp.transpose(buddy.reshape(3, rows, width), (1, 0, 2))
    parity = jnp.transpose(parity, (1, 0, 2))
    return (*(a.reshape(rows, width) for a in (w, m, v)), buddy, parity)


def solution(mesh):
    rows = P(("group", "domain"), None)
    blocks = P(("group", "domain"), None, None)
    return jax.shard_map(
        shards,
        mesh=mesh,
        in_specs=(rows, rows, rows, rows, P(), P()),
        out_specs=(rows, rows, rows, blocks, blocks),
        check_vma=False,
    )
```

time: 243 us -> 96.6 us (0.40)
  waiting for transfers between devices: 157 us -> 0 us
  Pallas kernels: 0 us -> 95.8 us
  local copies, waits for them, and re-layouts: 36.5 us -> 0 us
  other arithmetic: 31.6 us -> 0 us
  between operations: 14.8 us -> 0.66 us
    unnamed x2 -> x0, waiting for transfers between devices: 157 us -> none
    pallas_call x0 -> x4, Pallas kernels: none -> 95.8 us  [the longest x2 90.6 us: exchange(): pl.pallas_call((loading_kernel, second_kernel)[phase], out_shape=((whole,...]
    another operation x4 -> x0, local copies, waits for them, and re-layouts: 13.8 us -> none  [shards(): packed = jnp.stack([weight_new, moment1_new, moment2_new], axis=1)]
    gather x4 -> x0, local copies, waits for them, and re-layouts: 12.6 us -> none  [the longest x1 10.6 us: shards(): selected = jnp.take(packed, sources, axis=0)]
    unnamed x14 -> x0, local copies, waits for them, and re-layouts: 9.35 us -> none
    mul x1 -> x0, other arithmetic: 9.06 us -> none  [shards(): selected * jnp.take(scales, owners_of)[:, None, None]]
    another operation x1 -> x0, other arithmetic: 6.41 us -> none  [shards(): packed = jnp.stack([weight_new, moment1_new, moment2_new], axis=1)]
    select_n x3 -> x0, other arithmetic: 5.23 us -> none  [the longest x1 5.21 us: shards(): jnp.take(scales, owners_of)[:, None, None]]
  transfers between devices with their start and end apart: 2 -> 0, of which waited for: 1 -> 0; matrix products, arithmetic and copies ran while one was open for 5% -> 0% of each run, Pallas kernels for 0% -> 0%
where the time goes in v6:
time: 96.6 us; the launch traced here: 96.5 us
  Pallas kernels  95.8 us (99%)
    pallas_call x2, Pallas kernels, exchange(): pl.pallas_call((loading_kernel, second_kernel)[phase], out_shape=((whole,...  90.6 us
    pallas_call x1, Pallas kernels, middle(): pl.pallas_call(middle_kernel, out_shape=(one, one, one, jax.ShapeDtypeStr...  3.36 us

profile of v6, /device:TPU:0, one launch (start us, length us, event | category | flops | bytes accessed | tf_op | source)
XLA Modules:
  0.0 96.5 jit_solution(2247679733634258478)
XLA Ops:
  0.6 50.4 %exchange_one.1 = (f32[3,8,8,7168]{3,2,1,0:T(8,128)S(1)}, f32[3,8,8,7168]{3,2,1,0:T(8,128)S(1)}, f32[3,8,7168]{2,1,0:T(8,128)S(1)}, f32[3,8,7168]{2,1,0:T(8,128)S(1)}) custom-call(s32[8,16]{1,0:T(8,128)} %bitcast.15, s32[8]{0:T(128)} %exponents_in.1, f32[8,8,7168]{2,1,0:T(8,128)} %bitcast.12, f32[8,8,7168]{2,1,0:T(8,128)} %bitcast.13, ...), custom_call_target="tpu_custom_call" | custom-call | tf_op jit(solution)/shard_map/exchange_one/pallas_call | solution.py:396
  51.0 3.4 %middle.1 = (f32[8,8,7168]{2,1,0:T(8,128)}, f32[8,8,7168]{2,1,0:T(8,128)}, f32[8,8,7168]{2,1,0:T(8,128)}, f32[3,8,8,7168]{3,2,1,0:T(8,128)}, f32[8,128]{1,0:T(8,128)S(1)}) custom-call(f32[3,8,8,7168]{3,2,1,0:T(8,128)S(1)} %get-tuple-element.18.fresh, f32[3,8,8,7168]{3,2,1,0:T(8,128)S(1)} %get-tuple-element.19.buddy), custom_call_target="tpu_custom_call" | custom-call | tf_op jit(solution)/shard_map/middle/pallas_call | solution.py:445
  54.4 40.2 %exchange_two.1 = (f32[3,8,8,7168]{3,2,1,0:T(8,128)S(1)}, f32[3,8,7168]{2,1,0:T(8,128)S(1)}) custom-call(f32[3,8,8,7168]{3,2,1,0:T(8,128)S(1)} %get-tuple-element.18.fresh, f32[8,128]{1,0:T(8,128)S(1)} %get-tuple-element.23.after, f32[3,8,7168]{2,1,0:T(8,128)S(1)} %get-tuple-element.24.part_ref, f32[3,8,7168]{2,1,0:T(8,128)S(1)} %get-tuple-element.25.cross_ref), custom_call_target="tpu_custom_call" | custom-call | tf_op jit(solution)/shard_map/exchange_two/pallas_call | solution.py:396
  94.6 1.8 %finish.1 = (f32[3,8,8,7168]{3,2,1,0:T(8,128)}, f32[3,8,7168]{2,1,0:T(8,128)}) custom-call(f32[3,8,8,7168]{3,2,1,0:T(8,128)S(1)} %get-tuple-element.26.buddy, f32[3,8,7168]{2,1,0:T(8,128)S(1)} %get-tuple-element.27.parity, f32[3,8,8,7168]{3,2,1,0:T(8,128)} %get-tuple-element.28.buddy_in), custom_call_target="tpu_custom_call", output_to_operand_aliasing={{0}: (2, {})} | custom-call | tf_op jit(solution)/shard_map/finish/pallas_call | solution.py:462

commit v7 on v6

--- a/solution.py
+++ b/solution.py
@@ -149,10 +149,11 @@
     greet(y_plus, y_minus)
 
     corner = y == 0
+    beside = (x_plus, x_minus) if phase == 0 else ()
 
     @pl.when(corner)
     def _():
-        greet(x_plus, x_minus)
+        greet(*beside)
 
         @pl.when(z < ZS - 1)
         def _():
@@ -171,12 +172,12 @@
 
     @pl.when(corner & (z == 0))
     def _():
-        pl.semaphore_wait(barrier, 5)
+        pl.semaphore_wait(barrier, 3 + len(beside))
         greet(z_minus)
 
     @pl.when(corner & (z > 0))
     def _():
-        pl.semaphore_wait(barrier, 6)
+        pl.semaphore_wait(barrier, 4 + len(beside))
 
     @pl.when(corner & (z == ZS - 1))
     def _():
@@ -194,8 +195,8 @@
         @pl.when(y == 0)
         def _():
             pl.semaphore_wait(ring_sem.at[0], 1)
-            greet(x_plus, x_minus, z_plus, z_minus, semaphore=ring_sem.at[1])
-            pl.semaphore_wait(ring_sem.at[1], 4)
+            greet(*beside, z_plus, z_minus, semaphore=ring_sem.at[1])
+            pl.semaphore_wait(ring_sem.at[1], 2 + len(beside))
             greet(y_plus, y_minus, semaphore=ring_sem.at[2])
 
         @pl.when(y > 0)
@@ -266,10 +267,10 @@
 
         def all_of(c):
             start_all(hops(c, 0) + short(c))
+            pass_on(c, 0)
             meet_the_rest()
             out_plus.start()
             out_minus.start()
-            pass_on(c, 0)
             pass_on(c, 1)
             totals()
             end(c)

time: 96.6 us -> 96.3 us (level)
  no operation moved by 1% of the time
where the time goes in v7:
time: 96.3 us; the launch traced here: 96.2 us
  Pallas kernels  95.5 us (99%)
    pallas_call x2, Pallas kernels, exchange(): pl.pallas_call((loading_kernel, second_kernel)[phase], out_shape=((whole,...  90.3 us
    pallas_call x1, Pallas kernels, middle(): pl.pallas_call(middle_kernel, out_shape=(one, one, one, jax.ShapeDtypeStr...  3.36 us

profile of v7, /device:TPU:0, one launch (start us, length us, event | category | flops | bytes accessed | tf_op | source)
XLA Modules:
  0.0 96.2 jit_solution(4671451220926361721)
XLA Ops:
  0.6 50.4 %exchange_one.1 = (f32[3,8,8,7168]{3,2,1,0:T(8,128)S(1)}, f32[3,8,8,7168]{3,2,1,0:T(8,128)S(1)}, f32[3,8,7168]{2,1,0:T(8,128)S(1)}, f32[3,8,7168]{2,1,0:T(8,128)S(1)}) custom-call(s32[8,16]{1,0:T(8,128)} %bitcast.15, s32[8]{0:T(128)} %exponents_in.1, f32[8,8,7168]{2,1,0:T(8,128)} %bitcast.12, f32[8,8,7168]{2,1,0:T(8,128)} %bitcast.13, ...), custom_call_target="tpu_custom_call" | custom-call | tf_op jit(solution)/shard_map/exchange_one/pallas_call | solution.py:397
  51.0 3.4 %middle.1 = (f32[8,8,7168]{2,1,0:T(8,128)}, f32[8,8,7168]{2,1,0:T(8,128)}, f32[8,8,7168]{2,1,0:T(8,128)}, f32[3,8,8,7168]{3,2,1,0:T(8,128)}, f32[8,128]{1,0:T(8,128)S(1)}) custom-call(f32[3,8,8,7168]{3,2,1,0:T(8,128)S(1)} %get-tuple-element.18.fresh, f32[3,8,8,7168]{3,2,1,0:T(8,128)S(1)} %get-tuple-element.19.buddy), custom_call_target="tpu_custom_call" | custom-call | tf_op jit(solution)/shard_map/middle/pallas_call | solution.py:446
  54.4 40.0 %exchange_two.1 = (f32[3,8,8,7168]{3,2,1,0:T(8,128)S(1)}, f32[3,8,7168]{2,1,0:T(8,128)S(1)}) custom-call(f32[3,8,8,7168]{3,2,1,0:T(8,128)S(1)} %get-tuple-element.18.fresh, f32[8,128]{1,0:T(8,128)S(1)} %get-tuple-element.23.after, f32[3,8,7168]{2,1,0:T(8,128)S(1)} %get-tuple-element.24.part_ref, f32[3,8,7168]{2,1,0:T(8,128)S(1)} %get-tuple-element.25.cross_ref), custom_call_target="tpu_custom_call" | custom-call | tf_op jit(solution)/shard_map/exchange_two/pallas_call | solution.py:397
  94.4 1.8 %finish.1 = (f32[3,8,8,7168]{3,2,1,0:T(8,128)}, f32[3,8,7168]{2,1,0:T(8,128)}) custom-call(f32[3,8,8,7168]{3,2,1,0:T(8,128)S(1)} %get-tuple-element.26.buddy, f32[3,8,7168]{2,1,0:T(8,128)S(1)} %get-tuple-element.27.parity, f32[3,8,8,7168]{3,2,1,0:T(8,128)} %get-tuple-element.28.buddy_in), custom_call_target="tpu_custom_call", output_to_operand_aliasing={{0}: (2, {})} | custom-call | tf_op jit(solution)/shard_map/finish/pallas_call | solution.py:463

commit v8 on v6

--- a/solution.py
+++ b/solution.py
@@ -21,8 +21,8 @@
     (((0, 512), (512, 2304), (2816, 2304)), ((5120, 1024), (6144, 1024))),
 )
 SHORT = (
-    (((0, 0, 512), (0, 512, 6656), (1, 0, 3584)), ((1, 3584, 3584), (2, 0, 7168))),
-    (((0, 0, 512), (0, 512, 6656), (1, 0, 7168), (2, 0, 1024)), ((2, 1024, 6144),)),
+    (((0, 0, 512), (0, 512, 6656), (1, 0, 3584)), ((1, 3584, 3584), (2, 0, 3584), (2, 3584, 3584))),
+    (((0, 0, 512), (0, 512, 6656), (1, 0, 7168), (2, 0, 1024)), ((2, 1024, 3072), (2, 4096, 3072))),
 )
 F32 = jnp.float32
 DMA = pltpu.SemaphoreType.DMA

time: 96.6 us -> 96.6 us (level)
  no operation moved by 1% of the time
where the time goes in v8:
time: 96.6 us; the launch traced here: 96.5 us
  Pallas kernels  95.8 us (99%)
    pallas_call x2, Pallas kernels, exchange(): pl.pallas_call((loading_kernel, second_kernel)[phase], out_shape=((whole,...  90.6 us
    pallas_call x1, Pallas kernels, middle(): pl.pallas_call(middle_kernel, out_shape=(one, one, one, jax.ShapeDtypeStr...  3.36 us

profile of v8, /device:TPU:0, one launch (start us, length us, event | category | flops | bytes accessed | tf_op | source)
XLA Modules:
  0.0 96.5 jit_solution(7433036323474763342)
XLA Ops:
  0.6 50.4 %exchange_one.1 = (f32[3,8,8,7168]{3,2,1,0:T(8,128)S(1)}, f32[3,8,8,7168]{3,2,1,0:T(8,128)S(1)}, f32[3,8,7168]{2,1,0:T(8,128)S(1)}, f32[3,8,7168]{2,1,0:T(8,128)S(1)}) custom-call(s32[8,16]{1,0:T(8,128)} %bitcast.15, s32[8]{0:T(128)} %exponents_in.1, f32[8,8,7168]{2,1,0:T(8,128)} %bitcast.12, f32[8,8,7168]{2,1,0:T(8,128)} %bitcast.13, ...), custom_call_target="tpu_custom_call" | custom-call | tf_op jit(solution)/shard_map/exchange_one/pallas_call | solution.py:396
  51.0 3.4 %middle.1 = (f32[8,8,7168]{2,1,0:T(8,128)}, f32[8,8,7168]{2,1,0:T(8,128)}, f32[8,8,7168]{2,1,0:T(8,128)}, f32[3,8,8,7168]{3,2,1,0:T(8,128)}, f32[8,128]{1,0:T(8,128)S(1)}) custom-call(f32[3,8,8,7168]{3,2,1,0:T(8,128)S(1)} %get-tuple-element.18.fresh, f32[3,8,8,7168]{3,2,1,0:T(8,128)S(1)} %get-tuple-element.19.buddy), custom_call_target="tpu_custom_call" | custom-call | tf_op jit(solution)/shard_map/middle/pallas_call | solution.py:445
  54.4 40.3 %exchange_two.1 = (f32[3,8,8,7168]{3,2,1,0:T(8,128)S(1)}, f32[3,8,7168]{2,1,0:T(8,128)S(1)}) custom-call(f32[3,8,8,7168]{3,2,1,0:T(8,128)S(1)} %get-tuple-element.18.fresh, f32[8,128]{1,0:T(8,128)S(1)} %get-tuple-element.23.after, f32[3,8,7168]{2,1,0:T(8,128)S(1)} %get-tuple-element.24.part_ref, f32[3,8,7168]{2,1,0:T(8,128)S(1)} %get-tuple-element.25.cross_ref), custom_call_target="tpu_custom_call" | custom-call | tf_op jit(solution)/shard_map/exchange_two/pallas_call | solution.py:396
  94.6 1.8 %finish.1 = (f32[3,8,8,7168]{3,2,1,0:T(8,128)}, f32[3,8,7168]{2,1,0:T(8,128)}) custom-call(f32[3,8,8,7168]{3,2,1,0:T(8,128)S(1)} %get-tuple-element.26.buddy, f32[3,8,7168]{2,1,0:T(8,128)S(1)} %get-tuple-element.27.parity, f32[3,8,8,7168]{3,2,1,0:T(8,128)} %get-tuple-element.28.buddy_in), custom_call_target="tpu_custom_call", output_to_operand_aliasing={{0}: (2, {})} | custom-call | tf_op jit(solution)/shard_map/finish/pallas_call | solution.py:462
